TPU v7x, 32 devices: a whole 2x2x4 slice. The times are simulated.
32 devices in a mesh: batch: 8 (over z, x), tensor: 4 (over y, core).
Axes of the slice: x: 2, y: 2, z: 4, core: 2. Of those that a mesh axis runs over, the one named last changes fastest.
Arguments:
- tokens: bfloat16 [2048, 4096], P(('batch', 'tensor')), may hold values from -6 to 6
- norm_gain: float32 [4096], replicated, may hold values from 0.1 to 1.9
- w_query: bfloat16 [4096, 4096], P(None, 'tensor'), may hold values from -0.09375 to 0.09375
- w_key: bfloat16 [4096, 1024], P(None, 'tensor'), may hold values from -0.25 to 0.25
- w_value: bfloat16 [4096, 1024], P(None, 'tensor'), may hold values from -0.09375 to 0.09375
- w_out: bfloat16 [4096, 4096], P('tensor'), may hold values from -0.25 to 0.25
- prefix_keys: bfloat16 [4096, 1024], P('batch', 'tensor'), may hold values from -6 to 6
- prefix_values: bfloat16 [4096, 1024], P('batch', 'tensor'), may hold values from -6 to 6
- cache_keys: bfloat16 [36864, 1024], P('batch', 'tensor'), may hold values from -160 to 160
- cache_values: bfloat16 [36864, 1024], P('batch', 'tensor'), may hold values from -6 to 6
- cache_lengths: int32 [32], replicated, may hold values from 128 to 2048, as said below
- prefix_used: int32 [32], P('batch'), may hold values from 1024 to 4096
- parents: int32 [32, 64], P('batch'), may hold values from 0 to 62, as said below
- accepted_index: int32 [32, 8], P('batch'), may hold values from 0 to 63, as said below
Outputs:
- mixed_output: bfloat16 [2048, 4096], P(('batch', 'tensor'))
- accepted_keys: bfloat16 [32, 8, 1024], P('batch', None, 'tensor')
- accepted_values: bfloat16 [32, 8, 1024], P('batch', None, 'tensor')
Inputs may be any that keep to these rules, and one draw needn't show every extreme that they name: `cache_lengths`: within each aligned group of 4 requests at most 2 have more than 256 cached tokens; in the first group exactly that many do, and some request has exactly 2048. parents[r, 0] = 0; for i >= 1, parents[r, i] lies between max(0, i - 8) and i - 1. `accepted_index`: each row lists 8 tree positions, each the parent of the next, ending at a position of 32 or more; where the root is reached the row repeats 0 at its front.
All inputs are finite; a program needn't handle non-finite values.
Results may differ from a plain program's by a relative error of at most 0.015.
The roundings to bfloat16 on the way count: a program that leaves them out, or rounds other values in their place, can miss the bound.
Values may be sent and summed in bfloat16 or wider, within the bound.
No kernel may reach another device: no remote copies, remote signals or barrier semaphores. Data moves between devices by JAX's collectives and lax.ppermute only.
A program may use at most 192 MiB of HBM per device.

v0:
```python
import jax
import jax.numpy as jnp
from jax import lax
from jax.sharding import PartitionSpec as P

HD = 128


NEG_FILL = -1e30
HIGHEST = lax.Precision.HIGHEST


def rms_normed(tokens, norm_gain):
    values = tokens.astype(jnp.float32)
    factor = lax.rsqrt(jnp.mean(values * values, axis=-1, keepdims=True) + 1e-05)
    return (values * factor * norm_gain).astype(jnp.bfloat16)


def ancestor_table(parents):
    node_count = parents.shape[-1]
    column = jnp.arange(node_count, dtype=jnp.int32)
    linked = (parents[..., None] == column).astype(jnp.float32)
    itself = (column[:, None] == column[None, :]).astype(jnp.float32)
    ancestry = jnp.minimum(linked + itself, 1.0)
    for repeat in range(node_count.bit_length()):
        ancestry = jnp.minimum(
            jnp.einsum("rij,rjk->rik", ancestry, ancestry, precision=HIGHEST), 1.0
        )
    return ancestry


def rotate(values, positions):
    half_width = values.shape[-1] // 2
    frequency = 10000.0 ** (-jnp.arange(half_width, dtype=jnp.float32) / half_width)
    angles = positions.astype(jnp.float32)[:, None] * frequency[None, :]
    cosine = jnp.cos(angles)[:, None, :]
    sine_table = jnp.sin(angles)[:, None, :]
    first_half = values[..., :half_width]
    second_half = values[..., half_width:]
    return jnp.concatenate(
        [
            first_half * cosine - second_half * sine_table,
            second_half * cosine + first_half * sine_table,
        ],
        axis=-1,
    )


def absorb(carry, scores, visible, apply_values):
    running_max, running_sum, running_out = carry
    masked = jnp.where(visible, scores, NEG_FILL)
    new_max = jnp.maximum(running_max, jnp.max(masked, axis=-1))
    weights = jnp.where(visible, jnp.exp(masked - new_max[..., None]), 0.0)
    factor = jnp.exp(running_max - new_max)
    new_sum = running_sum * factor + jnp.sum(weights, axis=-1)
    new_out = running_out * factor[..., None] + apply_values(weights.astype(jnp.bfloat16))
    return (new_max, new_sum, new_out)


def combine(first_part, second_part):
    joint_max = jnp.maximum(first_part[0], second_part[0])
    first_factor = jnp.exp(first_part[0] - joint_max)
    second_factor = jnp.exp(second_part[0] - joint_max)
    joint_sum = first_part[1] * first_factor + second_part[1] * second_factor
    joint_out = first_part[2] * first_factor[..., None] + second_part[2] * second_factor[..., None]
    return (joint_max, joint_sum, joint_out)


def empty_partials(leading, head_size):
    return (
        jnp.full(leading, NEG_FILL, jnp.float32),
        jnp.zeros(leading, jnp.float32),
        jnp.zeros(leading + (head_size,), jnp.float32),
    )


def cache_partials(queries, all_keys, all_values, lower_slot, upper_slot, score_scale):
    capacity = all_keys.shape[0]
    block_size = min(512, capacity)
    kv_local = queries.shape[1]
    head_size = queries.shape[3]

    def one_request(request_items):
        request_query, lower_bound, upper_bound = request_items
        blocks = (upper_bound - lower_bound + block_size - 1) // block_size

        def block_step(block_index, carry):
            block_begin = lower_bound + block_index * block_size
            start = jnp.clip(block_begin, 0, capacity - block_size)
            block_keys = lax.dynamic_slice_in_dim(all_keys, start, block_size, 0).reshape(
                block_size, kv_local, head_size
            )
            block_values = lax.dynamic_slice_in_dim(all_values, start, block_size, 0).reshape(
                block_size, kv_local, head_size
            )
            slot_ids = start + jnp.arange(block_size, dtype=jnp.int32)
            visible = (slot_ids >= block_begin) & (
                slot_ids < jnp.minimum(upper_bound, block_begin + block_size)
            )
            scores = (
                jnp.einsum(
                    "hqd,khd->hqk", request_query, block_keys, preferred_element_type=jnp.float32
                )
                * score_scale
            )
            return absorb(
                carry,
                scores,
                visible[None, None, :],
                lambda rounded: jnp.einsum(
                    "hqk,khd->hqd", rounded, block_values, preferred_element_type=jnp.float32
                ),
            )

        start_carry = empty_partials(request_query.shape[:2], head_size)
        return lax.fori_loop(0, blocks, block_step, start_carry)

    return lax.map(one_request, (queries, lower_slot, upper_slot))


def body(
    tokens,
    norm_gain,
    w_query,
    w_key,
    w_value,
    w_out,
    prefix_keys,
    prefix_values,
    cache_keys,
    cache_values,
    cache_lengths,
    prefix_used,
    parents,
    accepted_index,
):
    req_count, tree_size = parents.shape
    head_size = HD
    query_cols = w_query.shape[1]
    key_cols = w_key.shape[1]
    kv_local = key_cols // head_size
    group_size = query_cols // key_cols
    query_rows = tree_size * group_size
    score_scale = head_size ** (-0.5)
    normed = rms_normed(tokens, norm_gain)
    piece = lax.all_gather(normed, "tensor", axis=0, tiled=True)
    projected = jnp.concatenate(
        [
            jnp.dot(piece, w_query, preferred_element_type=jnp.float32),
            jnp.dot(piece, w_key, preferred_element_type=jnp.float32),
            jnp.dot(piece, w_value, preferred_element_type=jnp.float32),
        ],
        axis=1,
    )
    group_index = lax.axis_index("batch")
    own_lengths = lax.dynamic_slice_in_dim(cache_lengths, group_index * req_count, req_count)
    ancestry = ancestor_table(parents)
    tree_depth = (jnp.sum(ancestry, axis=-1) - 1.0).astype(jnp.int32)
    position = ((prefix_used + own_lengths)[:, None] + tree_depth).reshape(req_count * tree_size)
    queries = rotate(
        projected[:, :query_cols].reshape(-1, kv_local * group_size, head_size), position
    ).astype(jnp.bfloat16)
    queries = queries.reshape(req_count, tree_size, kv_local, group_size, head_size).transpose(
        0, 2, 1, 3, 4
    )
    queries = queries.reshape(req_count, kv_local, query_rows, head_size)
    new_keys = rotate(
        projected[:, query_cols : query_cols + key_cols].reshape(-1, kv_local, head_size), position
    ).astype(jnp.bfloat16)
    new_keys = new_keys.reshape(req_count, tree_size, key_cols)
    new_values = (
        projected[:, query_cols + key_cols :]
        .astype(jnp.bfloat16)
        .reshape(req_count, tree_size, key_cols)
    )
    accepted_keys = jnp.take_along_axis(new_keys, accepted_index[:, :, None], axis=1)
    accepted_values = jnp.take_along_axis(new_values, accepted_index[:, :, None], axis=1)
    tree_keys = new_keys.reshape(req_count, tree_size, kv_local, head_size)
    tree_values = new_values.reshape(req_count, tree_size, kv_local, head_size)
    tree_scores = (
        jnp.einsum("rhqd,rkhd->rhqk", queries, tree_keys, preferred_element_type=jnp.float32)
        * score_scale
    )
    tree_visible = jnp.repeat(ancestry > 0.5, group_size, axis=1)[:, None]
    tree_part = absorb(
        empty_partials((req_count, kv_local, query_rows), head_size),
        tree_scores,
        tree_visible,
        lambda rounded: jnp.einsum(
            "rhqk,rkhd->rhqd", rounded, tree_values, preferred_element_type=jnp.float32
        ),
    )
    own_offsets = jnp.cumsum(own_lengths) - own_lengths
    cache_part = cache_partials(
        queries, cache_keys, cache_values, own_offsets, own_offsets + own_lengths, score_scale
    )
    local_part = combine(tree_part, cache_part)
    piece_keys = lax.all_gather(prefix_keys, "batch", axis=0, tiled=True)
    piece_values = lax.all_gather(prefix_values, "batch", axis=0, tiled=True)
    row_count = piece_keys.shape[0]
    shaped_keys = piece_keys.reshape(row_count, kv_local, head_size)
    shaped_values = piece_values.reshape(row_count, kv_local, head_size)
    slot_ids = jnp.arange(row_count, dtype=jnp.int32)
    visible = (slot_ids[None, :] < prefix_used[:, None])[:, None, None, :]
    scores = (
        jnp.einsum("rhqd,khd->rhqk", queries, shaped_keys, preferred_element_type=jnp.float32)
        * score_scale
    )
    folded = absorb(
        local_part,
        scores,
        visible,
        lambda rounded: jnp.einsum(
            "rhqk,khd->rhqd", rounded, shaped_values, preferred_element_type=jnp.float32
        ),
    )
    attended = (folded[2] / folded[1][..., None]).astype(jnp.bfloat16)
    attended = attended.reshape(req_count, kv_local, tree_size, group_size, head_size).transpose(
        0, 2, 1, 3, 4
    )
    attended = attended.reshape(req_count * tree_size, query_cols)
    mixed_rows = lax.psum_scatter(
        jnp.dot(attended, w_out, preferred_element_type=jnp.float32).astype(jnp.bfloat16),
        "tensor",
        scatter_dimension=0,
        tiled=True,
    )
    return (mixed_rows, accepted_keys, accepted_values)


def solution(mesh):
    in_specs = (
        P(("batch", "tensor"), None),
        P(),
        P(None, "tensor"),
        P(None, "tensor"),
        P(None, "tensor"),
        P("tensor", None),
        P("batch", "tensor"),
        P("batch", "tensor"),
        P("batch", "tensor"),
        P("batch", "tensor"),
        P(),
        P("batch"),
        P("batch", None),
        P("batch", None),
    )
    out_specs = (
        P(("batch", "tensor"), None),
        P("batch", None, "tensor"),
        P("batch", None, "tensor"),
    )
    return jax.shard_map(body, mesh=mesh, in_specs=in_specs, out_specs=out_specs, check_vma=False)
```

profile of v0, /device:TPU:0, one launch (start us, length us, event | category | flops | bytes accessed | tf_op | source)
XLA Modules:
  0.0 200.4 jit_solution(11750316172523123288)
XLA Ops:
  7.2 1.4 fusion.28
  8.6 2.0 %fusion.30 = bf16[64,4096]{1,0:T(8,128)(2,1)} fusion(bf16[64,4096]{1,0:T(8,128)(2,1)} %param.20, f32[4096]{0:T(1024)} %param.21, f32[64]{0:T(128)S(1)} %add_rsqrt_fusion), kind=kLoop, calls=%fused_computation.58 | loop fusion | flops 1048576 | bytes 1065216 | tf_op jit(solution)/shard_map/convert_element_type | solution.py:16
  10.7 1.8 copy.101
  12.6 1.8 copy.106
  14.5 0.7 dynamic-slice_bitcast_fusion.1
  15.4 0.7 iota_compare_fusion.2
  16.2 0.8 bitcast_subtract_fusion.1
  16.9 1.1 convolution_minimum_fusion.6
  20.8 4.7 %copy.100 = bf16[4608,256]{0,1:T(8,128)(2,1)} copy(bf16[4608,256]{1,0:T(8,128)(2,1)} %param.29) | data formatting | bytes 4718592 | tf_op jit(solution)/shard_map/while | solution.py:118
  25.5 4.4 %copy.99 = bf16[4608,256]{0,1:T(8,128)(2,1)} copy(bf16[4608,256]{1,0:T(8,128)(2,1)} %param.28) | data formatting | bytes 4718592 | tf_op jit(solution)/shard_map/while | solution.py:118
  29.9 6.4 %all-gather.4.cloned.1.call-done = bf16[256,4096]{1,0:T(8,128)(2,1)} async-done(((bf16[64,4096]{1,0:T(8,128)(2,1)}), bf16[256,4096]{1,0:T(8,128)(2,1)}) %all-gather.4.cloned.1.call-update) | async-done | bytes 2097168 | tf_op jit(solution)/shard_map/all_gather | solution.py:146
  36.2 6.3 %convolution_bitcast_fusion = f32[32,8,8,128]{3,1,2,0:T(8,128)S(1)} fusion(bf16[256,4096]{1,0:T(8,128)(2,1)} %all-gather.4.cloned.1.call-done, bf16[4096,1024]{1,0:T(8,128)(2,1)} %param.22), kind=kOutput, calls=%fused_computation.36 | convolution fusion | flops 2147483648 | bytes 11534336 | tf_op jit(solution)/shard_map/dot_general | solution.py:149
  42.8 0.5 subtract_convert_fusion
  43.3 0.7 pad_maximum_fusion
  44.3 1.0 fusion.57
  45.9 52.5 %while.69 = (s32[]{:T(128)}, f32[4,2,256]{2,1,0:T(2,128)S(1)}, f32[4,2,256]{2,1,0:T(2,128)S(1)}, f32[4,2,256,128]{3,2,1,0:T(8,128)}, s32[4]{0:T(128)S(1)}, /*ind...) while((s32[]{:T(128)}, f32[4,2,256]{2,1,0:T(2,128)S(1)}, ...), condition=%wide.region_9.10_spmd, body=%wide.region_4.9_spmd.sunk | while | flops 136711184 | bytes 6470884 | solution.py:118
  45.9 0.6 dynamic_slice.53
  46.5 0.7 dynamic_slice.54
  48.6 3.9 %while.70 = (s32[]{:T(128)}, f32[2,256]{1,0:T(2,128)S(1)}, f32[2,256]{1,0:T(2,128)S(1)}, f32[2,256,128]{2,1,0:T(8,128)S(1)}, s32[]{:T(128)}, /*index=5*/s32[]{:T...) while((s32[]{:T(128)}, f32[2,256]{1,0:T(2,128)S(1)}, ...), condition=%wide.region_8.8_spmd, body=%wide.region_5.7_spmd.sunk | while | flops 136711168 | bytes 5408989 | solution.py:116
  49.9 1.3 constant_dynamic-slice_fusion.3
  51.9 0.5 convolution_add_fusion.3
  52.5 0.7 bitcast_dynamic-update-slice_fusion.6
  53.2 0.6 dynamic_slice.53
  53.8 0.7 dynamic_slice.54
  55.9 15.5 %while.70 = (s32[]{:T(128)}, f32[2,256]{1,0:T(2,128)S(1)}, f32[2,256]{1,0:T(2,128)S(1)}, f32[2,256,128]{2,1,0:T(8,128)S(1)}, s32[]{:T(128)}, /*index=5*/s32[]{:T...) while((s32[]{:T(128)}, f32[2,256]{1,0:T(2,128)S(1)}, ...), condition=%wide.region_8.8_spmd, body=%wide.region_5.7_spmd.sunk | while | flops 136711168 | bytes 5408989 | solution.py:116
  57.2 1.4 constant_dynamic-slice_fusion.3
  59.2 0.5 convolution_add_fusion.3
  61.1 1.3 constant_dynamic-slice_fusion.3
  63.1 0.5 convolution_add_fusion.3
  65.0 1.3 constant_dynamic-slice_fusion.3
  67.0 0.5 convolution_add_fusion.3
  68.9 1.3 constant_dynamic-slice_fusion.3
  70.8 0.5 convolution_add_fusion.3
  71.4 0.8 bitcast_dynamic-update-slice_fusion.6
  72.1 0.6 dynamic_slice.53
  72.7 0.7 dynamic_slice.54
  74.8 3.9 %while.70 = (s32[]{:T(128)}, f32[2,256]{1,0:T(2,128)S(1)}, f32[2,256]{1,0:T(2,128)S(1)}, f32[2,256,128]{2,1,0:T(8,128)S(1)}, s32[]{:T(128)}, /*index=5*/s32[]{:T...) while((s32[]{:T(128)}, f32[2,256]{1,0:T(2,128)S(1)}, ...), condition=%wide.region_8.8_spmd, body=%wide.region_5.7_spmd.sunk | while | flops 136711168 | bytes 5408989 | solution.py:116
  76.2 1.4 constant_dynamic-slice_fusion.3
  78.2 0.5 convolution_add_fusion.3
  78.7 0.7 bitcast_dynamic-update-slice_fusion.6
  79.5 0.6 dynamic_slice.53
  80.0 0.7 dynamic_slice.54
  82.1 15.5 %while.70 = (s32[]{:T(128)}, f32[2,256]{1,0:T(2,128)S(1)}, f32[2,256]{1,0:T(2,128)S(1)}, f32[2,256,128]{2,1,0:T(8,128)S(1)}, s32[]{:T(128)}, /*index=5*/s32[]{:T...) while((s32[]{:T(128)}, f32[2,256]{1,0:T(2,128)S(1)}, ...), condition=%wide.region_8.8_spmd, body=%wide.region_5.7_spmd.sunk | while | flops 136711168 | bytes 5408989 | solution.py:116
  83.5 1.4 constant_dynamic-slice_fusion.3
  85.5 0.5 convolution_add_fusion.3
  87.4 1.3 constant_dynamic-slice_fusion.3
  89.3 0.5 convolution_add_fusion.3
  91.3 1.3 constant_dynamic-slice_fusion.3
  93.2 0.5 convolution_add_fusion.3
  95.1 1.3 constant_dynamic-slice_fusion.3
  97.1 0.5 convolution_add_fusion.3
  97.6 0.7 bitcast_dynamic-update-slice_fusion.6
  98.4 2.9 %convolution_convert_fusion.1 = bf16[256,256]{1,0:T(8,128)(2,1)S(1)} fusion(bf16[256,4096]{1,0:T(8,128)(2,1)} %all-gather.4.cloned.1.call-done, bf16[4096,256]{1,0:T(8,128)(2,1)} %param.24), kind=kOutput, calls=%fused_computation.48 | convolution fusion | flops 536936448 | bytes 4325376 | tf_op jit(solution)/shard_map/dot_general | solution.py:151
  101.4 0.4 fusion.56
  101.8 15.3 %bitcast_reduce_fusion = (f32[4,2,256]{2,0,1:T(4,128)S(1)}, f32[2,4,256,4096]{3,2,1,0:T(8,128)}) fusion(pred[4,4096]{1,0:T(4,128)(4,1)S(1)} %iota_compare_fusion.2, bf16[4096,2,128,1]{0,2,3,1:T(8,128)(2,1)} %bitcast.123, bf16[4,2,256,128]{3,2,1,0:T(8,128)(2,1)S(1)} %get-tuple-element.636), kind=kOutput, calls=%fused_computation.26 | convolution fusion | flops 2172647424 | bytes 36200448 | tf_op jit(solution)/shard_map/rhqd,khd->rhqk/dot_general | solution.py:206
  117.2 22.2 %fusion.14 = (f32[4,2,256]{2,0,1:T(4,128)S(1)}, bf16[4,2,256,4096]{3,2,0,1:T(8,128)(2,1)}) fusion(f32[2,4,256,4096]{3,2,1,0:T(8,128)} %get-tuple-element.367, f32[4,2,256]{2,0,1:T(4,128)S(1)} %copy.105, pred[4,4096]{1,0:T(4,128)(4,1)S(1)} %iota_compare_fusion.2), kind=kLoop, calls=%fused_computation.30 | loop fusion | flops 50329600 | bytes 50364416 | tf_op jit(solution)/shard_map/reduce_sum | solution.py:55
  139.5 1.4 all-gather.8.cloned.1.call-done
  140.9 11.8 %fusion.18 = f32[4,2,256,128]{3,2,1,0:T(8,128)} fusion(bf16[4096,2,128,1]{0,2,1,3:T(8,128)(2,1)} %bitcast.132, bf16[4,2,256,4096]{3,2,0,1:T(8,128)(2,1)} %get-tuple-element.348), kind=kOutput, calls=%fused_computation.35 | convolution fusion | flops 2147483648 | bytes 19922944 | tf_op jit(solution)/shard_map/rhqk,khd->rhqd/dot_general | solution.py:213
  152.7 3.6 %fusion.26 = bf16[4,2,256,128]{3,2,1,0:T(8,128)(2,1)S(1)} fusion(f32[4,2,256,128]{3,2,1,0:T(8,128)} %fusion.18, f32[4,2,256,128]{3,2,1,0:T(8,128)} %get-tuple-element.268, f32[4,2,256]{2,1,0:T(2,128)S(1)} %get-tuple-element.337, f32[4,2,256]{2,1,0:T(2,128)S(1)} %get-tuple-element.340, f32[4,2,256]{2,1,0:T(2,128)S(1)} %get-tuple-element.339, ...), kind=kOutput, calls=%fused_computation.45 | convolution fusion | flops 36044800 | bytes 3391488 | tf_op jit(solution)/shard_map/rhqk,rkhd->rhqd/dot_general | solution.py:189
  156.9 7.2 %convolution_convert_fusion = bf16[256,4096]{1,0:T(8,128)(2,1)} fusion(bf16[256,1024]{1,0:T(8,128)(2,1)S(1)} %reshape.219, bf16[1024,4096]{1,0:T(8,128)(2,1)} %param.25), kind=kOutput, calls=%fused_computation.34 | convolution fusion | flops 2148532224 | bytes 11010048 | tf_op jit(solution)/shard_map/dot_general | solution.py:223
  164.5 0.7 gather_fusion
  165.1 0.7 gather_fusion.1
  165.8 0.7 bitcast_select_fusion
  166.5 27.4 %reduce-scatter.2.cloned.1.call-done = bf16[64,4096]{1,0:T(8,128)(2,1)} async-done(((bf16[256,4096]{1,0:T(8,128)(2,1)}), bf16[64,4096]{1,0:T(8,128)(2,1)}) %reduce-scatter.2.cloned.1.call-update) | async-done | bytes 524304 | tf_op jit(solution)/shard_map/reduce_scatter | solution.py:222
  (138 shorter events, 11.4 us)
Async XLA Ops:
  7.2 37.1 %copy-start = (bf16[4096,256]{1,0:T(8,128)(2,1)S(1)}, bf16[4096,256]{1,0:T(8,128)(2,1)}, u32[]{:S(2)}) copy-start(bf16[4096,256]{1,0:T(8,128)(2,1)} %param.23) | copy-start | bytes 6291460
  7.2 29.1 %all-gather.4.cloned.1.call-start = ((), (), s32[]{:S(2)}) async-start(), calls=%async_computation.1 | async-start | bytes 2621440 | tf_op jit(solution)/shard_map/all_gather | solution.py:146
  10.7 91.1 %all-gather.6.cloned.1.call-start = ((), (), s32[]{:S(2)}) async-start(), calls=%async_computation.2 | async-start | bytes 2359296 | tf_op jit(solution)/shard_map/all_gather | solution.py:198
  12.6 128.3 %all-gather.8.cloned.1.call-start = ((), (), s32[]{:S(2)}) async-start(), calls=%async_computation.3 | async-start | bytes 2359296 | tf_op jit(solution)/shard_map/all_gather | solution.py:199
  14.4 179.5 %reduce-scatter.2.cloned.1.call-start = ((), (), s32[]{:S(2)}) async-start(), calls=%async_computation.4 | async-start | bytes 2621440 | tf_op jit(solution)/shard_map/reduce_scatter | solution.py:222
  42.6 1.7 copy-start.2
  156.9 7.3 %copy-start.3 = (s32[4,8]{1,0:T(4,128)S(1)}, s32[4,8]{1,0:T(4,128)}, u32[]{:S(2)}) copy-start(s32[4,8]{1,0:T(4,128)} %param.33) | copy-start | bytes 388
  156.9 37.0 %copy-start.1 = (bf16[4096,256]{1,0:T(8,128)(2,1)S(1)}, bf16[4096,256]{1,0:T(8,128)(2,1)}, u32[]{:S(2)}) copy-start(bf16[4096,256]{1,0:T(8,128)(2,1)} %param.23) | copy-start | bytes 6291460
Sparse Core Ops, SparseCore 0:
  10.8 25.3 all-gather.3
  38.3 51.1 all-gather.5
  91.5 49.2 all-gather.7
  164.2 29.6 reduce-scatter.1
where the time goes:
time: 202 us; the launch traced here: 200 us
  matrix products  60.1 us (30%)
  local copies, waits for them, and re-layouts  38.8 us (19%)
  waiting for transfers between devices  35.2 us (17%)
  other arithmetic  32.3 us (16%)
  loops' own time  19.7 us (10%)
  between operations  14.1 us (7%)
    reduce_scatter x1, waiting for transfers between devices, body(): lax.psum_scatter(jnp.dot(attended, w_out, preferred_element_type=jnp.floa...  27.4 us
    reduce_sum x12, other arithmetic, absorb(): new_sum = running_sum * factor + jnp.sum(weights, axis=-1)  24.5 us
    dot_general x1, matrix products, body(): jnp.einsum('rhqd,khd->rhqk', queries, shaped_keys, preferred_element_type...  15.3 us
    another operation x4, loops' own time, one_request(): return lax.fori_loop(0, blocks, block_step, start_carry)  14.1 us
    dynamic_slice x10, local copies, waits for them, and re-layouts, block_step(): lax.dynamic_slice_in_dim(all_values, start, block_size, 0)  13.5 us
    dot_general x1, matrix products, body(): jnp.einsum('rhqk,khd->rhqd', rounded, shaped_values, preferred_element_ty...  11.8 us
    while x2, local copies, waits for them, and re-layouts, cache_partials(): return lax.map(one_request, (queries, lower_slot, upper_slot))  9.07 us
    dot_general x1, matrix products, body(): jnp.dot(attended, w_out, preferred_element_type=jnp.float32)  7.2 us
  transfers between devices with their start and end apart: 4, of which 3 were waited for; matrix products, arithmetic and copies ran while one was open for 52% of the time, Pallas kernels for 0%

commit v1 on v0

v1 whole, which is shorter than its diff:
```python
import functools

import jax
import jax.numpy as jnp
from jax import lax
from jax.experimental import pallas as pl
from jax.experimental.pallas import tpu as pltpu
from jax.sharding import PartitionSpec as P

HD = 128
NEG_FILL = -1e30
LOG2E = 1.4426950408889634
AXES = ("batch", "tensor")
VMEM_LIMIT = 56 * 1024 * 1024


def params(**kw):
    return pltpu.CompilerParams(vmem_limit_bytes=VMEM_LIMIT, **kw)


def qkv_kernel(n_tok, steps, n_heads, kv_local, *refs):
    token_refs = refs[:n_tok]
    gain_ref, cos_ref, sin_ref, wq_ref, wk_ref, wv_ref = refs[n_tok : n_tok + 6]
    q_out, k_out, v_out = refs[n_tok + 6 : n_tok + 9]
    normed, acc = refs[n_tok + 9 :]
    step = pl.program_id(0)
    depth = wq_ref.shape[0]
    rows = token_refs[0].shape[0]
    q_cols = n_heads * HD
    k_cols = kv_local * HD

    @pl.when(step == 0)
    def _():
        for i, ref in enumerate(token_refs):
            values = ref[...].astype(jnp.float32)
            factor = lax.rsqrt(jnp.mean(values * values, axis=-1, keepdims=True) + 1e-05)
            scaled = (values * factor * gain_ref[...]).astype(jnp.bfloat16)
            for s in range(steps):
                normed[s, i * rows : (i + 1) * rows, :] = scaled[:, s * depth : (s + 1) * depth]

    x = normed[step]

    def part(lo, w_ref):
        width = w_ref.shape[1]
        d = jnp.dot(x, w_ref[...], preferred_element_type=jnp.float32)

        @pl.when(step == 0)
        def _():
            acc[:, lo : lo + width] = d

        @pl.when(step > 0)
        def _():
            acc[:, lo : lo + width] += d

    part(0, wq_ref)
    part(q_cols, wk_ref)
    part(q_cols + k_cols, wv_ref)

    @pl.when(step == steps - 1)
    def _():
        cosine = cos_ref[...]
        sine = sin_ref[...]
        reqs, tree = q_out.shape[0], q_out.shape[2]

        def rotated(lo):
            raw = acc[:, lo : lo + HD]
            return (raw * cosine + pltpu.roll(raw, HD // 2, 1) * sine).astype(jnp.bfloat16)

        for head in range(n_heads):
            out = rotated(head * HD)
            for r in range(reqs):
                q_out[r, head] = out[r * tree : (r + 1) * tree]
        for head in range(kv_local):
            k_out[:, head * HD : (head + 1) * HD] = rotated(q_cols + head * HD)
        v_out[...] = acc[:, q_cols + k_cols :].astype(jnp.bfloat16)


def project(token_list, gain, cosine, sine, w_query, w_key, w_value, reqs, tree):
    rows, width = token_list[0].shape
    total = rows * len(token_list)
    n_heads = w_query.shape[1] // HD
    kv_local = w_key.shape[1] // HD
    depth = min(512, width)
    steps = width // depth
    whole = lambda shape: pl.BlockSpec(shape, lambda s: (0,) * len(shape))
    return pl.pallas_call(
        functools.partial(qkv_kernel, len(token_list), steps, n_heads, kv_local),
        grid=(steps,),
        in_specs=[whole((rows, width)) for _ in token_list]
        + [whole((1, width)), whole((total, HD)), whole((total, HD))]
        + [pl.BlockSpec((depth, w.shape[1]), lambda s: (s, 0)) for w in (w_query, w_key, w_value)],
        out_specs=[
            whole((reqs, n_heads, tree, HD)),
            whole((total, w_key.shape[1])),
            whole((total, w_key.shape[1])),
        ],
        out_shape=[
            jax.ShapeDtypeStruct((reqs, n_heads, tree, HD), jnp.bfloat16),
            jax.ShapeDtypeStruct((total, w_key.shape[1]), jnp.bfloat16),
            jax.ShapeDtypeStruct((total, w_key.shape[1]), jnp.bfloat16),
        ],
        scratch_shapes=[
            pltpu.VMEM((steps, total, depth), jnp.bfloat16),
            pltpu.VMEM((total, w_query.shape[1] + 2 * w_key.shape[1]), jnp.float32),
        ],
        compiler_params=params(),
        cost_estimate=pl.CostEstimate(
            flops=2 * total * width * (w_query.shape[1] + 2 * w_key.shape[1]),
            bytes_accessed=2 * width * (w_query.shape[1] + 2 * w_key.shape[1]),
            transcendentals=0,
        ),
        name="project",
    )(*token_list, gain, cosine, sine, w_query, w_key, w_value)


def lane_max(t):
    return jnp.max(t, axis=1, keepdims=True)


def fold(q, k, v, bias, carry):
    scores = lax.dot_general(q, k, (((1,), (1,)), ((), ())), preferred_element_type=jnp.float32)
    t = scores * (HD**-0.5 * LOG2E) + bias
    keys = t.shape[1]
    rows = t.shape[0]
    m_block = jnp.broadcast_to(lane_max(t), (rows, HD))
    if carry is None:
        m_new = m_block
    else:
        m_old, l_old, acc_old = carry
        m_new = jnp.maximum(m_old, m_block)
    if keys % HD == 0:
        chunks = [jnp.exp2(t[:, j : j + HD] - m_new) for j in range(0, keys, HD)]
        total = chunks[0]
        for chunk in chunks[1:]:
            total = total + chunk
        p = jnp.concatenate([chunk.astype(jnp.bfloat16) for chunk in chunks], axis=1)
    else:
        p32 = jnp.exp2(t - m_new[:, :keys])
        total = jnp.broadcast_to(jnp.sum(p32, axis=1, keepdims=True), (rows, HD)) * (1.0 / HD)
        p = p32.astype(jnp.bfloat16)
    out = jnp.dot(p, v, preferred_element_type=jnp.float32)
    if carry is None:
        return m_new, total, out
    alpha = jnp.exp2(m_old - m_new)
    return m_new, l_old * alpha + total, acc_old * alpha + out


def cache_kernel(kv_local, block, lower, upper, q_ref, kn_ref, vn_ref, anc_ref, ck_ref, cv_ref, m_out, l_out, acc_out):
    r = pl.program_id(0)
    n_heads, tree = q_ref.shape[1], q_ref.shape[2]
    group = n_heads // kv_local
    rows = group * tree
    capacity = ck_ref.shape[0]
    bias = (anc_ref[0] - 1.0) * -NEG_FILL
    bias = jnp.concatenate([bias] * group, axis=0)
    for h in range(kv_local):
        cols = slice(h * HD, (h + 1) * HD)
        q = q_ref[0, h * group : (h + 1) * group].reshape(rows, HD)
        m, l, acc = fold(q, kn_ref[:, cols], vn_ref[:, cols], bias, None)
        m_out[0, h] = m
        l_out[0, h] = l
        acc_out[0, h] = acc
    low = lower[r]
    high = upper[r]
    first = (low // 16) * 16

    def step(i, _):
        begin = first + i * block
        start = pl.multiple_of(jnp.minimum(begin, capacity - block), 16)
        slots = start + lax.broadcasted_iota(jnp.int32, (1, block), 1)
        seen = (slots >= jnp.maximum(begin, low)) & (slots < high)
        mask = jnp.where(seen, 0.0, NEG_FILL)
        for h in range(kv_local):
            cols = slice(h * HD, (h + 1) * HD)
            q = q_ref[0, h * group : (h + 1) * group].reshape(rows, HD)
            k = ck_ref[pl.ds(start, block), cols]
            v = cv_ref[pl.ds(start, block), cols]
            m, l, acc = fold(q, k, v, mask, (m_out[0, h], l_out[0, h], acc_out[0, h]))
            m_out[0, h] = m
            l_out[0, h] = l
            acc_out[0, h] = acc
        return 0

    lax.fori_loop(0, (high - first + block - 1) // block, step, 0)


def state_shapes(reqs, kv_local, rows):
    return [jax.ShapeDtypeStruct((reqs, kv_local, rows, HD), jnp.float32)] * 3


def attend_cache(queries, new_keys, new_values, ancestry, cache_keys, cache_values, lower, upper, kv_local):
    reqs, n_heads, tree, _ = queries.shape
    rows = n_heads // kv_local * tree
    capacity, cols = cache_keys.shape
    block = min(512, capacity)
    state = pl.BlockSpec((1, kv_local, rows, HD), lambda r, *_: (r, 0, 0, 0))
    whole = pl.BlockSpec((capacity, cols), lambda r, *_: (0, 0))
    return pl.pallas_call(
        functools.partial(cache_kernel, kv_local, block),
        grid_spec=pltpu.PrefetchScalarGridSpec(
            num_scalar_prefetch=2,
            grid=(reqs,),
            in_specs=[
                pl.BlockSpec((1, n_heads, tree, HD), lambda r, *_: (r, 0, 0, 0)),
                pl.BlockSpec((tree, cols), lambda r, *_: (r, 0)),
                pl.BlockSpec((tree, cols), lambda r, *_: (r, 0)),
                pl.BlockSpec((1, tree, tree), lambda r, *_: (r, 0, 0)),
                whole,
                whole,
            ],
            out_specs=[state] * 3,
        ),
        out_shape=state_shapes(reqs, kv_local, rows),
        compiler_params=params(),
        cost_estimate=pl.CostEstimate(
            flops=4 * reqs * kv_local * rows * 1200 * HD, bytes_accessed=4 * capacity * cols, transcendentals=0
        ),
        name="attend_cache",
    )(lower, upper, queries, new_keys, new_values, ancestry, cache_keys, cache_values)


def prefix_kernel(kv_local, n_shards, final, bases, used, q_ref, *refs):
    r = pl.program_id(0)
    k_refs = refs[:n_shards]
    v_refs = refs[n_shards : 2 * n_shards]
    m_in, l_in, acc_in = refs[2 * n_shards : 2 * n_shards + 3]
    n_heads, tree = q_ref.shape[1], q_ref.shape[2]
    group = n_heads // kv_local
    rows = group * tree
    if final:
        out_ref, m_out, l_out, acc_out = refs[2 * n_shards + 3 :]
    else:
        m_out, l_out, acc_out = refs[2 * n_shards + 3 :]
    m_out[...] = m_in[...]
    l_out[...] = l_in[...]
    acc_out[...] = acc_in[...]
    for s in range(n_shards):
        count = k_refs[s].shape[0]
        visible = used[r] - bases[s]

        @pl.when(visible > 0)
        def _():
            slots = lax.broadcasted_iota(jnp.int32, (1, count), 1)
            mask = jnp.where(slots < visible, 0.0, NEG_FILL)
            for h in range(kv_local):
                cols = slice(h * HD, (h + 1) * HD)
                q = q_ref[0, h * group : (h + 1) * group].reshape(rows, HD)
                m, l, acc = fold(
                    q, k_refs[s][:, cols], v_refs[s][:, cols], mask, (m_out[0, h], l_out[0, h], acc_out[0, h])
                )
                m_out[0, h] = m
                l_out[0, h] = l
                acc_out[0, h] = acc

    if final:
        for h in range(kv_local):
            total = jnp.sum(l_out[0, h], axis=1, keepdims=True)
            result = (acc_out[0, h] / total).astype(jnp.bfloat16)
            for g in range(group):
                head = h * group + g
                out_ref[:, head * HD : (head + 1) * HD] = result[g * tree : (g + 1) * tree]


def attend_prefix(queries, keys, values, bases, used, state, kv_local, final):
    reqs, n_heads, tree, _ = queries.shape
    rows = n_heads // kv_local * tree
    n_shards = len(keys)
    spec = pl.BlockSpec((1, kv_local, rows, HD), lambda r, *_: (r, 0, 0, 0))
    count, cols = keys[0].shape
    shard = pl.BlockSpec((count, cols), lambda r, *_: (0, 0))
    if final:
        out_specs = pl.BlockSpec((tree, n_heads * HD), lambda r, *_: (r, 0))
        out_shape = jax.ShapeDtypeStruct((reqs * tree, n_heads * HD), jnp.bfloat16)
        scratch = [pltpu.VMEM((1, kv_local, rows, HD), jnp.float32)] * 3
        aliases = {}
    else:
        out_specs = [spec] * 3
        out_shape = state_shapes(reqs, kv_local, rows)
        scratch = []
        aliases = {3 + 2 * n_shards + i: i for i in range(3)}
    return pl.pallas_call(
        functools.partial(prefix_kernel, kv_local, n_shards, final),
        grid_spec=pltpu.PrefetchScalarGridSpec(
            num_scalar_prefetch=2,
            grid=(reqs,),
            in_specs=[pl.BlockSpec((1, n_heads, tree, HD), lambda r, *_: (r, 0, 0, 0))]
            + [shard] * (2 * n_shards)
            + [spec] * 3,
            out_specs=out_specs,
            scratch_shapes=scratch,
        ),
        out_shape=out_shape,
        input_output_aliases=aliases,
        compiler_params=params(),
        cost_estimate=pl.CostEstimate(
            flops=4 * reqs * kv_local * rows * n_shards * count * HD,
            bytes_accessed=2 * n_shards * count * cols * 2,
            transcendentals=0,
        ),
        name="attend_prefix",
    )(bases, used, queries, *keys, *values, *state)


def out_kernel(groups, x_ref, w_ref, *out_refs):
    product = jnp.dot(x_ref[...], w_ref[...], preferred_element_type=jnp.float32).astype(jnp.bfloat16)
    for out_ref, slots in zip(out_refs, groups):
        rows = out_ref.shape[1]
        for i, slot in enumerate(slots):
            out_ref[i] = product[slot * rows : (slot + 1) * rows]


def project_out(attended, w_out, groups, rows):
    depth, width = w_out.shape
    block = min(512, width)
    return pl.pallas_call(
        functools.partial(out_kernel, groups),
        grid=(width // block,),
        in_specs=[
            pl.BlockSpec(attended.shape, lambda j: (0, 0)),
            pl.BlockSpec((depth, block), lambda j: (0, j)),
        ],
        out_specs=[pl.BlockSpec((len(g), rows, block), lambda j: (0, 0, j)) for g in groups],
        out_shape=[jax.ShapeDtypeStruct((len(g), rows, width), jnp.bfloat16) for g in groups],
        compiler_params=params(),
        cost_estimate=pl.CostEstimate(
            flops=2 * attended.shape[0] * depth * width, bytes_accessed=2 * depth * width, transcendentals=0
        ),
        name="project_out",
    )(attended, w_out)


def ancestor_table(parents):
    node_count = parents.shape[-1]
    column = jnp.arange(node_count, dtype=jnp.int32)
    linked = (parents[..., None] == column) | (column[:, None] == column[None, :])
    ancestry = linked.astype(jnp.bfloat16)
    for repeat in range((node_count - 1).bit_length()):
        paths = jnp.einsum("rij,rjk->rik", ancestry, ancestry, preferred_element_type=jnp.float32)
        ancestry = jnp.minimum(paths, 1.0).astype(jnp.bfloat16)
    return ancestry.astype(jnp.float32)


def rotary_tables(position):
    half = HD // 2
    frequency = 10000.0 ** (-jnp.arange(half, dtype=jnp.float32) / half)
    angles = position.astype(jnp.float32)[:, None] * frequency[None, :]
    cosine = jnp.cos(angles)
    sine = jnp.sin(angles)
    return jnp.concatenate([cosine, cosine], axis=1), jnp.concatenate([-sine, sine], axis=1)


def swap_pairs(batch, tensor, move):
    columns = 2
    pairs = []
    for z in range(batch // columns):
        for x in range(columns):
            for t in range(tensor):
                z2, x2, t2 = move(z, x, t)
                pairs.append(((z * columns + x) * tensor + t, (z2 * columns + x2) * tensor + t2))
    return pairs


def body(
    sizes,
    tokens,
    norm_gain,
    w_query,
    w_key,
    w_value,
    w_out,
    prefix_keys,
    prefix_values,
    cache_keys,
    cache_values,
    cache_lengths,
    prefix_used,
    parents,
    accepted_index,
):
    batch, tensor = sizes
    reqs, tree = parents.shape
    kv_local = w_key.shape[1] // HD
    shard_rows = prefix_keys.shape[0]
    fast = sizes == (8, 4) and reqs == tensor and tokens.shape[0] == tree
    me_batch = lax.axis_index("batch")
    me_tensor = lax.axis_index("tensor")

    own_lengths = lax.dynamic_slice_in_dim(cache_lengths, me_batch * reqs, reqs)
    lower = jnp.cumsum(own_lengths) - own_lengths
    if fast:
        order = jnp.arange(reqs, dtype=jnp.int32) ^ me_tensor
        pick = order[:, None] == jnp.arange(reqs, dtype=jnp.int32)[None, :]
        sort1 = lambda a: jnp.sum(jnp.where(pick, a[None, :], 0), axis=1)
        own_lengths, lower, used = sort1(own_lengths), sort1(lower), sort1(prefix_used)
        tree_parents = jnp.sum(jnp.where(pick[:, :, None], parents[None], 0), axis=1)
    else:
        order = jnp.arange(reqs, dtype=jnp.int32)
        used = prefix_used
        tree_parents = parents

    if fast:
        pairs = functools.partial(swap_pairs, batch, tensor)
        core_pairs = pairs(lambda z, x, t: (z, x, t ^ 1))
        y_pairs = pairs(lambda z, x, t: (z, x, t ^ 2))
        x_pairs = pairs(lambda z, x, t: (z, 1 - x, t))
        z_pairs = pairs(lambda z, x, t: ((z + 1) % (batch // 2), x, t))
        send = lambda a, p: lax.ppermute(a, AXES, p)
        y_tokens = send(tokens, y_pairs)
        core_tokens = send(tokens, core_pairs)
        ring_keys, ring_values = [prefix_keys], [prefix_values]
        side_keys, side_values = [], []
        for s in range(batch // 2):
            if s < batch // 2 - 1:
                ring_keys.append(send(ring_keys[s], z_pairs))
                ring_values.append(send(ring_values[s], z_pairs))
            side_keys.append(send(ring_keys[s], x_pairs))
            side_values.append(send(ring_values[s], x_pairs))
        far_tokens = send(y_tokens, core_pairs)
        token_list = [tokens, core_tokens, y_tokens, far_tokens]
    else:
        gathered = lax.all_gather(tokens, "tensor", axis=0, tiled=True)
        token_list = [gathered]

    ancestry = ancestor_table(tree_parents)
    tree_depth = (jnp.sum(ancestry, axis=-1) - 1.0).astype(jnp.int32)
    position = ((used + own_lengths)[:, None] + tree_depth).reshape(reqs * tree)
    cosine, sine = rotary_tables(position)
    queries, new_keys, new_values = project(
        token_list, norm_gain[None, :], cosine, sine, w_query, w_key, w_value, reqs, tree
    )

    slot_of = jnp.arange(reqs, dtype=jnp.int32) ^ me_tensor if fast else order
    rows = (slot_of[:, None] * tree + accepted_index).reshape(-1)
    accepted_keys = jnp.take(new_keys, rows, axis=0).reshape(reqs, accepted_index.shape[1], -1)
    accepted_values = jnp.take(new_values, rows, axis=0).reshape(reqs, accepted_index.shape[1], -1)

    state = attend_cache(
        queries, new_keys, new_values, ancestry, cache_keys, cache_values, lower, lower + own_lengths, kv_local
    )
    if fast:
        z, x = me_batch // 2, me_batch % 2
        last = batch // 2 - 1
        for s in range(last + 1):
            home = (z - s) % (batch // 2)
            bases = jnp.stack([home * 2 + x, home * 2 + 1 - x]).astype(jnp.int32) * shard_rows
            state = attend_prefix(
                queries,
                [ring_keys[s], side_keys[s]],
                [ring_values[s], side_values[s]],
                bases,
                used,
                state,
                kv_local,
                s == last,
            )
        attended = state
        near, away = project_out(attended, w_out, ((0, 2), (1, 3)), tree)
        got = send(away, core_pairs)
        kept = near.astype(jnp.float32) + got.astype(jnp.float32)
        far = send(kept[1].astype(jnp.bfloat16), y_pairs)
        mixed_rows = (kept[0] + far.astype(jnp.float32)).astype(jnp.bfloat16)
    else:
        all_keys = lax.all_gather(prefix_keys, "batch", axis=0, tiled=True)
        all_values = lax.all_gather(prefix_values, "batch", axis=0, tiled=True)
        per_call = 4
        for s in range(0, batch, per_call):
            parts = range(s, min(s + per_call, batch))
            cut = lambda a: [a[i * shard_rows : (i + 1) * shard_rows] for i in parts]
            bases = jnp.array([i * shard_rows for i in parts], jnp.int32)
            state = attend_prefix(
                queries, cut(all_keys), cut(all_values), bases, used, state, kv_local, s + per_call >= batch
            )
        (partial,) = project_out(state, w_out, (tuple(range(reqs)),), tree)
        mixed_rows = lax.psum_scatter(
            partial.reshape(reqs * tree, -1), "tensor", scatter_dimension=0, tiled=True
        )
    return (mixed_rows, accepted_keys, accepted_values)


def solution(mesh):
    sizes = (mesh.shape["batch"], mesh.shape["tensor"])
    in_specs = (
        P(("batch", "tensor"), None),
        P(),
        P(None, "tensor"),
        P(None, "tensor"),
        P(None, "tensor"),
        P("tensor", None),
        P("batch", "tensor"),
        P("batch", "tensor"),
        P("batch", "tensor"),
        P("batch", "tensor"),
        P(),
        P("batch"),
        P("batch", None),
        P("batch", None),
    )
    out_specs = (
        P(("batch", "tensor"), None),
        P("batch", None, "tensor"),
        P("batch", None, "tensor"),
    )
    return jax.shard_map(
        functools.partial(body, sizes), mesh=mesh, in_specs=in_specs, out_specs=out_specs, check_vma=False
    )
```

time: 202 us -> 134 us (0.66)
  the two profiles are of different devices: /device:TPU:0 before, /device:TPU:26 now
where the time goes in v1:
time: 134 us; the launch traced here: 133 us
  Pallas kernels  74 us (55%)
  waiting for transfers between devices  23.3 us (17%)
  starting transfers between devices  15.7 us (12%)
  other arithmetic  11 us (8%)
  local copies, waits for them, and re-layouts  5.8 us (4%)
  matrix products  1.69 us (1%)
    pallas_call x4, Pallas kernels, attend_prefix(): pl.pallas_call(functools.partial(prefix_kernel, kv_local, n_shards, final...  36.4 us
    ppermute x19, waiting for transfers between devices, body(): send = lambda a, p: lax.ppermute(a, AXES, p)  23.3 us
    ppermute x19, starting transfers between devices, body(): send = lambda a, p: lax.ppermute(a, AXES, p)  15.7 us
    pallas_call x1, Pallas kernels, attend_cache(): pl.pallas_call(functools.partial(cache_kernel, kv_local, block), grid_spe...  14.5 us
    pallas_call x1, Pallas kernels, project(): pl.pallas_call(functools.partial(qkv_kernel, len(token_list), steps, n_he...  14.5 us
    pallas_call x1, Pallas kernels, project_out(): pl.pallas_call(functools.partial(out_kernel, groups), grid=(width // bloc...  8.68 us
    unnamed x44, local copies, waits for them, and re-layouts  2.87 us
  transfers between devices with their start and end apart: 19, of which 6 were waited for; matrix products, arithmetic and copies ran while one was open for 10% of the time, Pallas kernels for 42%

profile of v1, /device:TPU:26, one launch (start us, length us, event | category | flops | bytes accessed | tf_op | source)
XLA Modules:
  0.0 132.6 jit_solution(6315821406455599277)
XLA Ops:
  0.6 1.6 %collective-permute-start.1 = (bf16[64,4096]{1,0:T(8,128)(2,1)}, bf16[64,4096]{1,0:T(8,128)(2,1)S(1)}, u32[]{:S(2)}, u32[]{:S(2)}) collective-permute-start(bf16[64,4096]{1,0:T(8,128)(2,1)} %refs_0_.2), channel_id=1, source_target_pairs={{0,2},{1,3},{2,0},{3,1},{4,6},{5,7},{6,4},{7,5},{8,10},{9,11},{10,... | collective-permute-start | bytes 1572872 | tf_op jit(solution)/shard_map/ppermute | solution.py:407
  2.2 0.5 collective-permute-start.15
  2.8 0.2 collective-permute-start.3
  3.0 1.6 %collective-permute-start.7 = (bf16[512,256]{1,0:T(8,128)(2,1)}, bf16[512,256]{1,0:T(8,128)(2,1)S(1)}, u32[]{:S(2)}, u32[]{:S(2)}) collective-permute-start(bf16[512,256]{1,0:T(8,128)(2,1)} %refs_2_.1), channel_id=1, source_target_pairs={{0,8},{1,9},{2,10},{3,11},{4,12},{5,13},{6,14},{7,15},{8,16},{9,17... | collective-permute-start | bytes 786440 | tf_op jit(solution)/shard_map/ppermute | solution.py:407
  4.6 0.7 dynamic-slice_bitcast_fusion
  5.3 0.7 dynamic_slice.3
  6.1 0.2 reduce-window.9
  6.3 0.7 bitcast_subtract_fusion
  7.0 0.1 iota_compare_fusion.2
  7.1 0.8 select_reduce_fusion
  7.9 0.5 fusion.1
  8.3 0.3 fusion.3
  8.6 0.9 fusion.25
  9.6 0.7 add_multiply_fusion.3.bases
  10.2 0.7 add_multiply_fusion.2.bases
  10.9 0.9 select_reduce_fusion.1
  11.8 0.6 fusion.24
  12.3 0.1 add_convert_fusion
  12.4 0.6 add_multiply_fusion.1.bases
  13.0 0.1 convert_element_type.66
  13.1 1.5 %collective-permute-done.1.refs_2_ = bf16[64,4096]{1,0:T(8,128)(2,1)S(1)} collective-permute-done((bf16[64,4096]{1,0:T(8,128)(2,1)}, bf16[64,4096]{1,0:T(8,128)(2,1)S(1)}, u32[]{:S(2)}, u32[]{:S(2)}) %collective-permute-start.1) | collective-permute-done | bytes 524320 | tf_op jit(solution)/shard_map/ppermute | solution.py:407
  14.6 0.5 fusion.20
  15.1 0.3 collective-permute-start.4
  15.4 1.6 %collective-permute-done.7.refs_2_ = bf16[512,256]{1,0:T(8,128)(2,1)S(1)} collective-permute-done((bf16[512,256]{1,0:T(8,128)(2,1)}, bf16[512,256]{1,0:T(8,128)(2,1)S(1)}, u32[]{:S(2)}, u32[]{:S(2)}) %collective-permute-start.7) | collective-permute-done | bytes 262176 | tf_op jit(solution)/shard_map/ppermute | solution.py:407
  17.0 2.1 %collective-permute-start.8 = (bf16[512,256]{1,0:T(8,128)(2,1)S(1)}, bf16[512,256]{1,0:T(8,128)(2,1)S(1)}, u32[]{:S(2)}, u32[]{:S(2)}) collective-permute-start(bf16[512,256]{1,0:T(8,128)(2,1)S(1)} %collective-permute-done.7.refs_2_), channel_id=1, source_target_pairs={{0,8},{1,9},{2,10},{3,11},{4,12},{5,13},{6,14},{7,15},{8,16},{9,17... | collective-permute-start | bytes 786440 | tf_op jit(solution)/shard_map/ppermute | solution.py:407
  19.1 0.6 add_multiply_fusion.bases
  19.8 0.8 pad_maximum_fusion.refs_5_
  20.5 0.8 pad_maximum_fusion.1.refs_6_
  21.3 1.5 %collective-permute-start.16 = (bf16[512,256]{1,0:T(8,128)(2,1)}, bf16[512,256]{1,0:T(8,128)(2,1)S(1)}, u32[]{:S(2)}, u32[]{:S(2)}) collective-permute-start(bf16[512,256]{1,0:T(8,128)(2,1)} %refs_2_.1), channel_id=1, source_target_pairs={{0,4},{1,5},{2,6},{3,7},{4,0},{5,1},{6,2},{7,3},{8,12},{9,13},{10,... | collective-permute-start | bytes 786440 | tf_op jit(solution)/shard_map/ppermute | solution.py:407
  22.8 0.5 collective-permute-start.13
  23.3 1.0 collective-permute-done.4.refs_0_
  24.3 0.5 collective-permute-start.14
  24.8 4.7 %collective-permute-done.8.refs_2_ = bf16[512,256]{1,0:T(8,128)(2,1)S(1)} collective-permute-done((bf16[512,256]{1,0:T(8,128)(2,1)S(1)}, bf16[512,256]{1,0:T(8,128)(2,1)S(1)}, u32[]{:S(2)}, u32[]{:S(2)}) %collective-permute-start.8) | collective-permute-done | bytes 262176 | tf_op jit(solution)/shard_map/ppermute | solution.py:407
  29.5 2.1 %collective-permute-start.9 = (bf16[512,256]{1,0:T(8,128)(2,1)S(1)}, bf16[512,256]{1,0:T(8,128)(2,1)S(1)}, u32[]{:S(2)}, u32[]{:S(2)}) collective-permute-start(bf16[512,256]{1,0:T(8,128)(2,1)S(1)} %collective-permute-done.8.refs_2_), channel_id=1, source_target_pairs={{0,8},{1,9},{2,10},{3,11},{4,12},{5,13},{6,14},{7,15},{8,16},{9,17... | collective-permute-start | bytes 786440 | tf_op jit(solution)/shard_map/ppermute | solution.py:407
  31.6 0.2 collective-permute-start.5
  31.9 0.6 copy-done.2
  32.4 14.5 %project.1 = (bf16[4,8,64,128]{3,2,1,0:T(8,128)(2,1)}, bf16[256,256]{1,0:T(8,128)(2,1)}, bf16[256,256]{1,0:T(8,128)(2,1)}) custom-call(bf16[64,4096]{1,0:T(8,128)(2,1)} %refs_0_.2, bf16[64,4096]{1,0:T(8,128)(2,1)} %copy-done.1, bf16[64,4096]{1,0:T(8,128)(2,1)} %copy-done, bf16[64,4096]{1,0:T(8,128)(2,1)} %copy-done.2, f32[1,4096]{1,0:T(1,128)} %bitcast.29, ...), custom_call_target="tpu_custom_call" | custom-call | flops 3221225472 | bytes 12582912 | tf_op jit(solution)/shard_map/project/pallas_call | solution.py:86
  47.0 1.4 %collective-permute-start.11 = (bf16[512,256]{1,0:T(8,128)(2,1)S(1)}, bf16[512,256]{1,0:T(8,128)(2,1)S(1)}, u32[]{:S(2)}, u32[]{:S(2)}) collective-permute-start(bf16[512,256]{1,0:T(8,128)(2,1)S(1)} %collective-permute-done.4.refs_0_), channel_id=1, source_target_pairs={{0,4},{1,5},{2,6},{3,7},{4,0},{5,1},{6,2},{7,3},{8,12},{9,13},{10,... | collective-permute-start | bytes 786440 | tf_op jit(solution)/shard_map/ppermute | solution.py:407
  48.3 0.8 collective-permute-start.12
  49.1 14.5 %attend_cache.1 = (f32[4,2,256,128]{3,2,1,0:T(8,128)}, f32[4,2,256,128]{3,2,1,0:T(8,128)}, f32[4,2,256,128]{3,2,1,0:T(8,128)}) custom-call(s32[4]{0:T(128)} %copy-done.20, s32[4]{0:T(128)} %get-tuple-element.46.upper, bf16[4,8,64,128]{3,2,1,0:T(8,128)(2,1)} %get-tuple-element.21.q_ref, bf16[256,256]{1,0:T(8,128)(2,1)} %get-tuple-element.22.kn_ref, ...), custom_call_target="tpu_custom_call" | custom-call | flops 1258291200 | bytes 4718592 | tf_op jit(solution)/shard_map/attend_cache/pallas_call | solution.py:198
  63.7 1.4 %collective-permute-start.10 = (bf16[512,256]{1,0:T(8,128)(2,1)S(1)}, bf16[512,256]{1,0:T(8,128)(2,1)S(1)}, u32[]{:S(2)}, u32[]{:S(2)}) collective-permute-start(bf16[512,256]{1,0:T(8,128)(2,1)S(1)} %collective-permute-done.9.refs_2_), channel_id=1, source_target_pairs={{0,4},{1,5},{2,6},{3,7},{4,0},{5,1},{6,2},{7,3},{8,12},{9,13},{10,... | collective-permute-start | bytes 786440 | tf_op jit(solution)/shard_map/ppermute | solution.py:407
  65.0 0.7 collective-permute-start.6
  65.8 6.8 %attend_prefix.4 = (f32[4,2,256,128]{3,2,1,0:T(8,128)}, f32[4,2,256,128]{3,2,1,0:T(8,128)}, f32[4,2,256,128]{3,2,1,0:T(8,128)}) custom-call(s32[2]{0:T(128)} %add_multiply_fusion.3.bases, s32[4]{0:T(128)} %copy-done.19, bf16[4,8,64,128]{3,2,1,0:T(8,128)(2,1)} %get-tuple-element.21.q_ref, ...), custom_call_target="tpu_custom_call", output_to_operand_aliasing={{0}: (7, {}), {1}: (8, {}), {2}: (9, {})} | custom-call | flops 1073741824 | bytes 1048576 | tf_op jit(solution)/shard_map/attend_prefix/pallas_call | solution.py:281
  72.7 0.7 copy-done.13
  73.4 9.8 %attend_prefix.5 = (f32[4,2,256,128]{3,2,1,0:T(8,128)}, f32[4,2,256,128]{3,2,1,0:T(8,128)}, f32[4,2,256,128]{3,2,1,0:T(8,128)}) custom-call(s32[2]{0:T(128)} %add_multiply_fusion.2.bases, s32[4]{0:T(128)} %copy-done.19, bf16[4,8,64,128]{3,2,1,0:T(8,128)(2,1)} %get-tuple-element.21.q_ref, ...), custom_call_target="tpu_custom_call", output_to_operand_aliasing={{0}: (7, {}), {1}: (8, {}), {2}: (9, {})} | custom-call | flops 1073741824 | bytes 1048576 | tf_op jit(solution)/shard_map/attend_prefix/pallas_call | solution.py:281
  83.1 0.0 copy-start.15
  83.2 0.7 copy-done.15
  83.8 0.1 copy-done.16
  83.9 9.7 %attend_prefix.6 = (f32[4,2,256,128]{3,2,1,0:T(8,128)}, f32[4,2,256,128]{3,2,1,0:T(8,128)}, f32[4,2,256,128]{3,2,1,0:T(8,128)}) custom-call(s32[2]{0:T(128)} %add_multiply_fusion.1.bases, s32[4]{0:T(128)} %copy-done.19, bf16[4,8,64,128]{3,2,1,0:T(8,128)(2,1)} %get-tuple-element.21.q_ref, ...), custom_call_target="tpu_custom_call", output_to_operand_aliasing={{0}: (7, {}), {1}: (8, {}), {2}: (9, {})} | custom-call | flops 1073741824 | bytes 1048576 | tf_op jit(solution)/shard_map/attend_prefix/pallas_call | solution.py:281
  93.7 0.7 copy-done.17
  94.4 0.1 copy-done.18
  94.5 10.0 %attend_prefix.7.x_ref = bf16[256,1024]{1,0:T(8,128)(2,1)} custom-call(s32[2]{0:T(128)} %add_multiply_fusion.bases, s32[4]{0:T(128)} %copy-done.19, bf16[4,8,64,128]{3,2,1,0:T(8,128)(2,1)} %get-tuple-element.21.q_ref, bf16[512,256]{1,0:T(8,128)(2,1)} %copy-done.11, bf16[512,256]{1,0:T(8,128)(2,1)} %copy-done.18, bf16[512,256]{1,0:T(8,128)(2,1)} %copy-done.10, ...), custom_call_target="tpu_custom_call" | custom-call | flops 1073741824 | bytes 1048576 | tf_op jit(solution)/shard_map/attend_prefix/pallas_call | solution.py:281
  104.5 8.7 %project_out.1 = (bf16[2,64,4096]{2,1,0:T(8,128)(2,1)}, bf16[2,64,4096]{2,1,0:T(8,128)(2,1)}) custom-call(bf16[256,1024]{1,0:T(8,128)(2,1)} %attend_prefix.7.x_ref, bf16[1024,4096]{1,0:T(8,128)(2,1)} %w_ref.1), custom_call_target="tpu_custom_call" | custom-call | flops 2147483648 | bytes 8388608 | tf_op jit(solution)/shard_map/project_out/pallas_call | solution.py:315
  113.2 0.1 broadcast_add_fusion
  113.3 0.1 reshape.125
  113.4 2.7 %collective-permute-done.17 = bf16[2,64,4096]{2,1,0:T(8,128)(2,1)S(1)} collective-permute-done((bf16[2,64,4096]{2,1,0:T(8,128)(2,1)}, bf16[2,64,4096]{2,1,0:T(8,128)(2,1)S(1)}, u32[]{:S(2)}, u32[]{:S(2)}) %collective-permute-start.17) | collective-permute-done | bytes 1048608 | tf_op jit(solution)/shard_map/ppermute | solution.py:407
  116.1 1.5 %convert_add_fusion = f32[2,64,4096]{2,1,0:T(8,128)S(1)} fusion(bf16[2,64,4096]{2,1,0:T(8,128)(2,1)S(1)} %collective-permute-done.17, bf16[2,64,4096]{2,1,0:T(8,128)(2,1)} %get-tuple-element.36), kind=kLoop, calls=%fused_computation.2 | loop fusion | flops 1572864 | bytes 4194304 | tf_op jit(solution)/shard_map/add | solution.py:459
  117.6 0.1 fusion.9
  117.6 0.2 collective-permute-start.18
  117.9 0.6 gather_fusion
  118.5 0.6 gather_fusion.1
  119.2 0.7 select_bitcast_fusion
  119.9 11.8 %collective-permute-done.18 = bf16[64,4096]{1,0:T(8,128)(2,1)S(1)} collective-permute-done((bf16[64,4096]{1,0:T(8,128)(2,1)S(1)}, bf16[64,4096]{1,0:T(8,128)(2,1)S(1)}, u32[]{:S(2)}, u32[]{:S(2)}) %collective-permute-start.18) | collective-permute-done | bytes 524320 | tf_op jit(solution)/shard_map/ppermute | solution.py:407
  131.7 0.9 fusion.8
  (59 shorter events, 0.2 us)
Async XLA Ops:
  0.6 13.9 %collective-permute-start.1 = (bf16[64,4096]{1,0:T(8,128)(2,1)}, bf16[64,4096]{1,0:T(8,128)(2,1)S(1)}, u32[]{:S(2)}, u32[]{:S(2)}) collective-permute-start(bf16[64,4096]{1,0:T(8,128)(2,1)} %refs_0_.2), channel_id=1, source_target_pairs={{0,2},{1,3},{2,0},{3,1},{4,6},{5,7},{6,4},{7,5},{8,10},{9,11},{10,... | collective-permute-start | bytes 1572872 | tf_op jit(solution)/shard_map/ppermute | solution.py:407
  2.2 20.6 %collective-permute-start = (bf16[64,4096]{1,0:T(8,128)(2,1)}, bf16[64,4096]{1,0:T(8,128)(2,1)S(1)}, u32[]{:S(2)}, u32[]{:S(2)}) collective-permute-start(bf16[64,4096]{1,0:T(8,128)(2,1)} %refs_0_.2), channel_id=1, source_target_pairs={{0,1},{1,0},{2,3},{3,2},{4,5},{5,4},{6,7},{7,6},{8,9},{9,8},{10,11... | collective-permute-start | bytes 1572872 | tf_op jit(solution)/shard_map/ppermute | solution.py:407
  2.2 19.1 %collective-permute-start.15 = (bf16[512,256]{1,0:T(8,128)(2,1)}, bf16[512,256]{1,0:T(8,128)(2,1)S(1)}, u32[]{:S(2)}, u32[]{:S(2)}) collective-permute-start(bf16[512,256]{1,0:T(8,128)(2,1)} %refs_0_.3), channel_id=1, source_target_pairs={{0,4},{1,5},{2,6},{3,7},{4,0},{5,1},{6,2},{7,3},{8,12},{9,13},{10,... | collective-permute-start | bytes 786440 | tf_op jit(solution)/shard_map/ppermute | solution.py:407
  2.8 12.4 %collective-permute-start.3 = (bf16[512,256]{1,0:T(8,128)(2,1)}, bf16[512,256]{1,0:T(8,128)(2,1)S(1)}, u32[]{:S(2)}, u32[]{:S(2)}) collective-permute-start(bf16[512,256]{1,0:T(8,128)(2,1)} %refs_0_.3), channel_id=1, source_target_pairs={{0,8},{1,9},{2,10},{3,11},{4,12},{5,13},{6,14},{7,15},{8,16},{9,17... | collective-permute-start | bytes 786440 | tf_op jit(solution)/shard_map/ppermute | solution.py:407
  3.0 14.0 %collective-permute-start.7 = (bf16[512,256]{1,0:T(8,128)(2,1)}, bf16[512,256]{1,0:T(8,128)(2,1)S(1)}, u32[]{:S(2)}, u32[]{:S(2)}) collective-permute-start(bf16[512,256]{1,0:T(8,128)(2,1)} %refs_2_.1), channel_id=1, source_target_pairs={{0,8},{1,9},{2,10},{3,11},{4,12},{5,13},{6,14},{7,15},{8,16},{9,17... | collective-permute-start | bytes 786440 | tf_op jit(solution)/shard_map/ppermute | solution.py:407
  11.7 35.1 %copy-start.19 = (s32[4]{0:T(128)}, s32[4]{0:T(128)S(1)}, u32[]{:S(2)}) copy-start(s32[4]{0:T(128)S(1)} %get-tuple-element.39.used) | copy-start | bytes 52
  11.8 35.1 %copy-start.20 = (s32[4]{0:T(128)}, s32[4]{0:T(128)S(1)}, u32[]{:S(2)}) copy-start(s32[4]{0:T(128)S(1)} %get-tuple-element.38.lower) | copy-start | bytes 52
  14.6 17.3 %copy-start = (bf16[64,4096]{1,0:T(8,128)(2,1)}, bf16[64,4096]{1,0:T(8,128)(2,1)S(1)}, u32[]{:S(2)}) copy-start(bf16[64,4096]{1,0:T(8,128)(2,1)S(1)} %collective-permute-done.1.refs_2_) | copy-start | bytes 1572868
  14.6 17.0 %collective-permute-start.2 = (bf16[64,4096]{1,0:T(8,128)(2,1)S(1)}, bf16[64,4096]{1,0:T(8,128)(2,1)S(1)}, u32[]{:S(2)}, u32[]{:S(2)}) collective-permute-start(bf16[64,4096]{1,0:T(8,128)(2,1)S(1)} %collective-permute-done.1.refs_2_), channel_id=1, source_target_pairs={{0,1},{1,0},{2,3},{3,2},{4,5},{5,4},{6,7},{7,6},{8,9},{9,8},{10,11... | collective-permute-start | bytes 1572872 | tf_op jit(solution)/shard_map/ppermute | solution.py:407
  15.1 31.8 %copy-start.5 = (bf16[512,256]{1,0:T(8,128)(2,1)}, bf16[512,256]{1,0:T(8,128)(2,1)S(1)}, u32[]{:S(2)}) copy-start(bf16[512,256]{1,0:T(8,128)(2,1)S(1)} %collective-permute-done.3.refs_0_) | copy-start | bytes 786436
  15.1 9.2 %collective-permute-start.4 = (bf16[512,256]{1,0:T(8,128)(2,1)S(1)}, bf16[512,256]{1,0:T(8,128)(2,1)S(1)}, u32[]{:S(2)}, u32[]{:S(2)}) collective-permute-start(bf16[512,256]{1,0:T(8,128)(2,1)S(1)} %collective-permute-done.3.refs_0_), channel_id=1, source_target_pairs={{0,8},{1,9},{2,10},{3,11},{4,12},{5,13},{6,14},{7,15},{8,16},{9,17... | collective-permute-start | bytes 786440 | tf_op jit(solution)/shard_map/ppermute | solution.py:407
  17.0 29.9 %copy-start.6 = (bf16[512,256]{1,0:T(8,128)(2,1)}, bf16[512,256]{1,0:T(8,128)(2,1)S(1)}, u32[]{:S(2)}) copy-start(bf16[512,256]{1,0:T(8,128)(2,1)S(1)} %collective-permute-done.7.refs_2_) | copy-start | bytes 786436
  17.0 12.5 %collective-permute-start.8 = (bf16[512,256]{1,0:T(8,128)(2,1)S(1)}, bf16[512,256]{1,0:T(8,128)(2,1)S(1)}, u32[]{:S(2)}, u32[]{:S(2)}) collective-permute-start(bf16[512,256]{1,0:T(8,128)(2,1)S(1)} %collective-permute-done.7.refs_2_), channel_id=1, source_target_pairs={{0,8},{1,9},{2,10},{3,11},{4,12},{5,13},{6,14},{7,15},{8,16},{9,17... | collective-permute-start | bytes 786440 | tf_op jit(solution)/shard_map/ppermute | solution.py:407
  21.3 25.7 %copy-start.7 = (bf16[512,256]{1,0:T(8,128)(2,1)}, bf16[512,256]{1,0:T(8,128)(2,1)S(1)}, u32[]{:S(2)}) copy-start(bf16[512,256]{1,0:T(8,128)(2,1)S(1)} %collective-permute-done.15.refs_1_) | copy-start | bytes 786436
  21.3 25.7 %collective-permute-start.16 = (bf16[512,256]{1,0:T(8,128)(2,1)}, bf16[512,256]{1,0:T(8,128)(2,1)S(1)}, u32[]{:S(2)}, u32[]{:S(2)}) collective-permute-start(bf16[512,256]{1,0:T(8,128)(2,1)} %refs_2_.1), channel_id=1, source_target_pairs={{0,4},{1,5},{2,6},{3,7},{4,0},{5,1},{6,2},{7,3},{8,12},{9,13},{10,... | collective-permute-start | bytes 786440 | tf_op jit(solution)/shard_map/ppermute | solution.py:407
  22.8 9.1 %copy-start.1 = (bf16[64,4096]{1,0:T(8,128)(2,1)}, bf16[64,4096]{1,0:T(8,128)(2,1)S(1)}, u32[]{:S(2)}) copy-start(bf16[64,4096]{1,0:T(8,128)(2,1)S(1)} %collective-permute-done.refs_1_) | copy-start | bytes 1572868
  22.8 25.6 %collective-permute-start.13 = (bf16[512,256]{1,0:T(8,128)(2,1)S(1)}, bf16[512,256]{1,0:T(8,128)(2,1)S(1)}, u32[]{:S(2)}, u32[]{:S(2)}) collective-permute-start(bf16[512,256]{1,0:T(8,128)(2,1)S(1)} %collective-permute-done.3.refs_0_), channel_id=1, source_target_pairs={{0,4},{1,5},{2,6},{3,7},{4,0},{5,1},{6,2},{7,3},{8,12},{9,13},{10,... | collective-permute-start | bytes 786440 | tf_op jit(solution)/shard_map/ppermute | solution.py:407
  24.3 22.7 %copy-start.8 = (bf16[512,256]{1,0:T(8,128)(2,1)}, bf16[512,256]{1,0:T(8,128)(2,1)S(1)}, u32[]{:S(2)}) copy-start(bf16[512,256]{1,0:T(8,128)(2,1)S(1)} %collective-permute-done.4.refs_0_) | copy-start | bytes 786436
  24.3 48.3 %collective-permute-start.14 = (bf16[512,256]{1,0:T(8,128)(2,1)S(1)}, bf16[512,256]{1,0:T(8,128)(2,1)S(1)}, u32[]{:S(2)}, u32[]{:S(2)}) collective-permute-start(bf16[512,256]{1,0:T(8,128)(2,1)S(1)} %collective-permute-done.7.refs_2_), channel_id=1, source_target_pairs={{0,4},{1,5},{2,6},{3,7},{4,0},{5,1},{6,2},{7,3},{8,12},{9,13},{10,... | collective-permute-start | bytes 786440 | tf_op jit(solution)/shard_map/ppermute | solution.py:407
  29.5 18.8 %copy-start.9 = (bf16[512,256]{1,0:T(8,128)(2,1)}, bf16[512,256]{1,0:T(8,128)(2,1)S(1)}, u32[]{:S(2)}) copy-start(bf16[512,256]{1,0:T(8,128)(2,1)S(1)} %collective-permute-done.8.refs_2_) | copy-start | bytes 786436
  29.5 34.1 %collective-permute-start.9 = (bf16[512,256]{1,0:T(8,128)(2,1)S(1)}, bf16[512,256]{1,0:T(8,128)(2,1)S(1)}, u32[]{:S(2)}, u32[]{:S(2)}) collective-permute-start(bf16[512,256]{1,0:T(8,128)(2,1)S(1)} %collective-permute-done.8.refs_2_), channel_id=1, source_target_pairs={{0,8},{1,9},{2,10},{3,11},{4,12},{5,13},{6,14},{7,15},{8,16},{9,17... | collective-permute-start | bytes 786440 | tf_op jit(solution)/shard_map/ppermute | solution.py:407
  31.6 0.8 copy-start.2
  31.6 33.4 %collective-permute-start.5 = (bf16[512,256]{1,0:T(8,128)(2,1)S(1)}, bf16[512,256]{1,0:T(8,128)(2,1)S(1)}, u32[]{:S(2)}, u32[]{:S(2)}) collective-permute-start(bf16[512,256]{1,0:T(8,128)(2,1)S(1)} %collective-permute-done.4.refs_0_), channel_id=1, source_target_pairs={{0,8},{1,9},{2,10},{3,11},{4,12},{5,13},{6,14},{7,15},{8,16},{9,17... | collective-permute-start | bytes 786440 | tf_op jit(solution)/shard_map/ppermute | solution.py:407
  47.0 16.7 %copy-start.14 = (bf16[512,256]{1,0:T(8,128)(2,1)}, bf16[512,256]{1,0:T(8,128)(2,1)S(1)}, u32[]{:S(2)}) copy-start(bf16[512,256]{1,0:T(8,128)(2,1)S(1)} %collective-permute-done.16.refs_3_) | copy-start | bytes 786436
  47.0 36.2 %collective-permute-start.11 = (bf16[512,256]{1,0:T(8,128)(2,1)S(1)}, bf16[512,256]{1,0:T(8,128)(2,1)S(1)}, u32[]{:S(2)}, u32[]{:S(2)}) collective-permute-start(bf16[512,256]{1,0:T(8,128)(2,1)S(1)} %collective-permute-done.4.refs_0_), channel_id=1, source_target_pairs={{0,4},{1,5},{2,6},{3,7},{4,0},{5,1},{6,2},{7,3},{8,12},{9,13},{10,... | collective-permute-start | bytes 786440 | tf_op jit(solution)/shard_map/ppermute | solution.py:407
  48.3 15.3 %copy-start.12 = (bf16[512,256]{1,0:T(8,128)(2,1)}, bf16[512,256]{1,0:T(8,128)(2,1)S(1)}, u32[]{:S(2)}) copy-start(bf16[512,256]{1,0:T(8,128)(2,1)S(1)} %collective-permute-done.13.refs_1_) | copy-start | bytes 786436
  48.3 34.8 %collective-permute-start.12 = (bf16[512,256]{1,0:T(8,128)(2,1)S(1)}, bf16[512,256]{1,0:T(8,128)(2,1)S(1)}, u32[]{:S(2)}, u32[]{:S(2)}) collective-permute-start(bf16[512,256]{1,0:T(8,128)(2,1)S(1)} %collective-permute-done.8.refs_2_), channel_id=1, source_target_pairs={{0,4},{1,5},{2,6},{3,7},{4,0},{5,1},{6,2},{7,3},{8,12},{9,13},{10,... | collective-permute-start | bytes 786440 | tf_op jit(solution)/shard_map/ppermute | solution.py:407
  63.7 9.0 %copy-start.10 = (bf16[512,256]{1,0:T(8,128)(2,1)}, bf16[512,256]{1,0:T(8,128)(2,1)S(1)}, u32[]{:S(2)}) copy-start(bf16[512,256]{1,0:T(8,128)(2,1)S(1)} %collective-permute-done.9.refs_2_) | copy-start | bytes 786436
  63.7 30.0 %collective-permute-start.10 = (bf16[512,256]{1,0:T(8,128)(2,1)S(1)}, bf16[512,256]{1,0:T(8,128)(2,1)S(1)}, u32[]{:S(2)}, u32[]{:S(2)}) collective-permute-start(bf16[512,256]{1,0:T(8,128)(2,1)S(1)} %collective-permute-done.9.refs_2_), channel_id=1, source_target_pairs={{0,4},{1,5},{2,6},{3,7},{4,0},{5,1},{6,2},{7,3},{8,12},{9,13},{10,... | collective-permute-start | bytes 786440 | tf_op jit(solution)/shard_map/ppermute | solution.py:407
  65.0 7.6 %copy-start.11 = (bf16[512,256]{1,0:T(8,128)(2,1)}, bf16[512,256]{1,0:T(8,128)(2,1)S(1)}, u32[]{:S(2)}) copy-start(bf16[512,256]{1,0:T(8,128)(2,1)S(1)} %collective-permute-done.5.refs_0_) | copy-start | bytes 786436
  65.0 28.6 %collective-permute-start.6 = (bf16[512,256]{1,0:T(8,128)(2,1)S(1)}, bf16[512,256]{1,0:T(8,128)(2,1)S(1)}, u32[]{:S(2)}, u32[]{:S(2)}) collective-permute-start(bf16[512,256]{1,0:T(8,128)(2,1)S(1)} %collective-permute-done.5.refs_0_), channel_id=1, source_target_pairs={{0,4},{1,5},{2,6},{3,7},{4,0},{5,1},{6,2},{7,3},{8,12},{9,13},{10,... | collective-permute-start | bytes 786440 | tf_op jit(solution)/shard_map/ppermute | solution.py:407
  72.6 0.7 copy-start.13
  83.1 0.7 copy-start.15
  83.2 0.8 copy-start.16
  93.7 0.7 copy-start.17
  93.7 0.8 copy-start.18
  104.5 8.7 %copy-start.21 = (s32[4,8]{1,0:T(4,128)S(1)}, s32[4,8]{1,0:T(4,128)}, u32[]{:S(2)}) copy-start(s32[4,8]{1,0:T(4,128)} %param.29) | copy-start | bytes 388
  113.2 2.9 %collective-permute-start.17 = (bf16[2,64,4096]{2,1,0:T(8,128)(2,1)}, bf16[2,64,4096]{2,1,0:T(8,128)(2,1)S(1)}, u32[]{:S(2)}, u32[]{:S(2)}) collective-permute-start(bf16[2,64,4096]{2,1,0:T(8,128)(2,1)} %get-tuple-element.37), channel_id=1, source_target_pairs={{0,1},{1,0},{2,3},{3,2},{4,5},{5,4},{6,7},{7,6},{8,9},{9,8},{10,11... | collective-permute-start | bytes 3145736 | tf_op jit(solution)/shard_map/ppermute | solution.py:407
  116.1 1.8 %copy-start.4 = (bf16[256,256]{1,0:T(8,128)(2,1)S(1)}, bf16[256,256]{1,0:T(8,128)(2,1)}, u32[]{:S(2)}) copy-start(bf16[256,256]{1,0:T(8,128)(2,1)} %get-tuple-element.22.kn_ref) | copy-start | bytes 393220
  116.1 2.5 %copy-start.3 = (bf16[256,256]{1,0:T(8,128)(2,1)S(1)}, bf16[256,256]{1,0:T(8,128)(2,1)}, u32[]{:S(2)}) copy-start(bf16[256,256]{1,0:T(8,128)(2,1)} %get-tuple-element.23.vn_ref) | copy-start | bytes 393220
  117.6 14.0 %collective-permute-start.18 = (bf16[64,4096]{1,0:T(8,128)(2,1)S(1)}, bf16[64,4096]{1,0:T(8,128)(2,1)S(1)}, u32[]{:S(2)}, u32[]{:S(2)}) collective-permute-start(bf16[64,4096]{1,0:T(8,128)(2,1)S(1)} %fusion.9), channel_id=1, source_target_pairs={{0,2},{1,3},{2,0},{3,1},{4,6},{5,7},{6,4},{7,5},{8,10},{9,11},{10,... | collective-permute-start | bytes 1572872 | tf_op jit(solution)/shard_map/ppermute | solution.py:407

commit v2 on v0

v2 whole, which is shorter than its diff:
```python
import functools

import jax
import jax.numpy as jnp
from jax import lax
from jax.experimental import pallas as pl
from jax.experimental.pallas import tpu as pltpu
from jax.sharding import PartitionSpec as P

HD = 128
NEG_FILL = -1e30
LOG2E = 1.4426950408889634
AXES = ("batch", "tensor")
SCALE = HD**-0.5 * LOG2E
COST = 1.1e9
HBM = pl.BlockSpec(memory_space=pltpu.HBM)
VMEM = pl.BlockSpec(memory_space=pltpu.VMEM)
SMEM = pl.BlockSpec(memory_space=pltpu.SMEM)


def call(kernel, in_specs, args, out_shape, scratch, megabytes, microseconds, name, after=()):
    n_in, n_out = len(args), len(out_shape)

    def wrapped(*refs):
        kernel(*refs[:n_in], *refs[n_in + len(after) :])

    return pl.pallas_call(
        wrapped,
        in_specs=in_specs + [HBM] * len(after),
        out_specs=[VMEM] * n_out,
        out_shape=out_shape,
        scratch_shapes=scratch,
        compiler_params=pltpu.CompilerParams(vmem_limit_bytes=megabytes * 2**20),
        cost_estimate=pl.CostEstimate(flops=int(microseconds * COST), bytes_accessed=0, transcendentals=0),
        name=name,
    )(*args, *after)


def dot_nt(a, b):
    return lax.dot_general(a, b, (((1,), (1,)), ((), ())), preferred_element_type=jnp.float32)


def head_cols(h):
    return slice(h * HD, (h + 1) * HD)


def fetch_all(sources, held, sems):
    copies = [pltpu.make_async_copy(src, held.at[i], sems.at[i]) for i, src in enumerate(sources)]
    for copy in copies:
        copy.start()
    return copies


def qkv_kernel(n_tok, n_heads, kv_local, steps, *refs):
    token_refs = refs[:n_tok]
    gain_ref, cos_ref, sin_ref = refs[n_tok : n_tok + 3]
    weights = refs[n_tok + 3 : n_tok + 6]
    q_out, k_out, v_out, held, normed, acc, wq, wk, wv, sems, weight_sems = refs[n_tok + 6 :]
    copies = fetch_all(token_refs, held, sems)
    depth = wq.shape[0] // steps
    chunks = []
    for s in range(steps):
        span = slice(s * depth, (s + 1) * depth)
        chunks.append(
            [
                pltpu.make_async_copy(src.at[span], dst.at[span], weight_sems.at[s, i])
                for i, (src, dst) in enumerate(zip(weights, (wq, wk, wv)))
            ]
        )
        for copy in chunks[-1]:
            copy.start()
    rows = held.shape[1]
    step = min(16, rows)
    for i in range(n_tok):
        copies[i].wait()
        for lo in range(0, rows, step):
            values = held[i, lo : lo + step].astype(jnp.float32)
            factor = lax.rsqrt(jnp.mean(values * values, axis=-1, keepdims=True) + 1e-05)
            normed[i * rows + lo : i * rows + lo + step] = (values * factor * gain_ref[...]).astype(jnp.bfloat16)
    cosine = cos_ref[...]
    sine = sin_ref[...]
    reqs, tree = q_out.shape[0], q_out.shape[2]

    def rotated(raw):
        return (raw * cosine + pltpu.roll(raw, HD // 2, 1) * sine).astype(jnp.bfloat16)

    for s in range(steps):
        for copy in chunks[s]:
            copy.wait()
        span = slice(s * depth, (s + 1) * depth)
        x = normed[:, span]
        lo = 0
        for which, w in enumerate((wq, wk, wv)):
            width = w.shape[1]
            raw = jnp.dot(x, w[span], preferred_element_type=jnp.float32)
            if s > 0:
                raw = acc[:, lo : lo + width] + raw
            if s < steps - 1:
                acc[:, lo : lo + width] = raw
            elif which == 0:
                for head in range(n_heads):
                    out = rotated(raw[:, head_cols(head)])
                    for r in range(reqs):
                        q_out[r, head] = out[r * tree : (r + 1) * tree]
            elif which == 1:
                for head in range(kv_local):
                    k_out[:, head_cols(head)] = rotated(raw[:, head_cols(head)])
            else:
                v_out[...] = raw.astype(jnp.bfloat16)
            lo += width


def project(token_list, gain, cosine, sine, w_query, w_key, w_value, tree, after=()):
    rows, width = token_list[0].shape
    n_tok = len(token_list)
    total = rows * n_tok
    n_heads = w_query.shape[1] // HD
    cols = w_key.shape[1]
    steps = 4
    return call(
        functools.partial(qkv_kernel, n_tok, n_heads, cols // HD, steps),
        [HBM] * n_tok + [VMEM] * 3 + [HBM] * 3,
        [*token_list, gain, cosine, sine, w_query, w_key, w_value],
        [
            jax.ShapeDtypeStruct((total // tree, n_heads, tree, HD), jnp.bfloat16),
            jax.ShapeDtypeStruct((total, cols), jnp.bfloat16),
            jax.ShapeDtypeStruct((total, cols), jnp.bfloat16),
        ],
        [
            pltpu.VMEM((n_tok, rows, width), jnp.bfloat16),
            pltpu.VMEM((total, width), jnp.bfloat16),
            pltpu.VMEM((total, w_query.shape[1] + 2 * cols), jnp.float32),
            pltpu.VMEM(w_query.shape, jnp.bfloat16),
            pltpu.VMEM(w_key.shape, jnp.bfloat16),
            pltpu.VMEM(w_value.shape, jnp.bfloat16),
            pltpu.SemaphoreType.DMA((n_tok,)),
            pltpu.SemaphoreType.DMA((steps, 3)),
        ],
        50,
        7,
        "project",
        after,
    )


def absorb(carry, scores, biases, v):
    chunks = []
    for s, bias in zip(scores, biases):
        s = s + bias
        chunks += [s[:, j : j + HD] for j in range(0, s.shape[1], HD)]
    top = chunks[0]
    for c in chunks[1:]:
        top = jnp.maximum(top, c)
    m_new = jnp.broadcast_to(jnp.max(top, axis=1, keepdims=True) * SCALE, top.shape)
    if carry is not None:
        m_new = jnp.maximum(carry[0], m_new)
    total = None
    rounded = []
    for c in chunks:
        w = jnp.exp2(c * SCALE - m_new)
        total = w if total is None else total + w
        rounded.append(w.astype(jnp.bfloat16))
    out = jnp.dot(jnp.concatenate(rounded, axis=1), v, preferred_element_type=jnp.float32)
    if carry is not None:
        alpha = jnp.exp2(carry[0] - m_new)
        total = carry[1] * alpha + total
        out = carry[2] * alpha + out
    return m_new, total, out


def fold_heads(q_ref, slot, kv_local, keys, values, bias, load, store):
    group, tree = q_ref.shape[1] // kv_local, q_ref.shape[2]
    rows = group * tree

    def scores_of(h):
        q = q_ref[slot, h * group : (h + 1) * group].reshape(rows, HD)
        return [dot_nt(q, k(h)) for k in keys]

    def values_of(h):
        parts = [v(h) for v in values]
        return parts[0] if len(parts) == 1 else jnp.concatenate(parts, axis=0)

    ahead = scores_of(0)
    for h in range(kv_local):
        now = ahead
        if h + 1 < kv_local:
            ahead = scores_of(h + 1)
        store(h, absorb(load(h), now, bias, values_of(h)))


def state_access(refs, r):
    def load(h):
        return tuple(ref[r, h] for ref in refs)

    def store(h, state):
        for ref, value in zip(refs, state):
            ref[r, h] = value

    return load, store


def fold_shards(q_ref, r, offset, kv_local, used, bases, base0, held, groups, states):
    n = held.shape[0] // 2
    count = held.shape[1]
    load, store = state_access(states, r)
    for group in groups:
        visible = [used - bases[base0 + i] for i in group]
        most = visible[0]
        for other in visible[1:]:
            most = jnp.maximum(most, other)

        @pl.when(most > 0)
        def _():
            slots = lax.broadcasted_iota(jnp.int32, (1, count), 1)
            fold_heads(
                q_ref,
                offset + r,
                kv_local,
                [lambda h, i=i: held[i, :, head_cols(h)] for i in group],
                [lambda h, i=i: held[n + i, :, head_cols(h)] for i in group],
                [jnp.where(slots < v, 0.0, NEG_FILL) for v in visible],
                load,
                store,
            )


def pairs_of(n):
    return [tuple(range(i, min(i + 2, n))) for i in range(0, n, 2)]


def first_kernel(kv_local, near, block, n_shards, offset, groups, base0, info, bases, q_ref, kn_ref, vn_ref, anc_ref, ck_ref, cv_ref, *refs):
    sources = refs[: 2 * n_shards]
    m_out, l_out, acc_out, k_near, v_near, held, sems = refs[-7:]
    states = (m_out, l_out, acc_out)
    copies = fetch_all(sources, held, sems)
    reqs = m_out.shape[0]
    n_heads, tree = q_ref.shape[1:3]
    group = n_heads // kv_local
    capacity = ck_ref.shape[0]
    for r in range(reqs):
        load, store = state_access(states, r)
        low = info[0, offset + r]
        high = info[1, offset + r]
        start0 = pl.multiple_of(jnp.minimum((low // 16) * 16, capacity - near), 16)
        k_near[0:tree] = kn_ref[(offset + r) * tree : (offset + r + 1) * tree]
        v_near[0:tree] = vn_ref[(offset + r) * tree : (offset + r + 1) * tree]
        k_near[tree : tree + near] = ck_ref[pl.ds(start0, near), :]
        v_near[tree : tree + near] = cv_ref[pl.ds(start0, near), :]
        column = lax.broadcasted_iota(jnp.int32, (tree, tree + near), 1)
        slots = column - tree + start0
        seen = ((slots >= low) & (slots < high)).astype(jnp.float32)
        linked = jnp.concatenate([anc_ref[offset + r], jnp.zeros((tree, tree + near - HD), jnp.float32)], axis=1)
        bias = jnp.where(jnp.where(column < tree, linked, seen) > 0.5, 0.0, NEG_FILL)
        bias = jnp.concatenate([bias] * group, axis=0)
        fold_heads(
            q_ref,
            offset + r,
            kv_local,
            [lambda h: k_near[:, head_cols(h)]],
            [lambda h: v_near[:, head_cols(h)]],
            [bias],
            lambda h: None,
            store,
        )
        begin0 = start0 + near

        def step(i, _):
            begin = begin0 + i * block
            start = pl.multiple_of(jnp.minimum(begin, capacity - block), 16)
            place = start + lax.broadcasted_iota(jnp.int32, (1, block), 1)
            mask = jnp.where((place >= begin) & (place < high), 0.0, NEG_FILL)
            fold_heads(
                q_ref,
                offset + r,
                kv_local,
                [lambda h: ck_ref[pl.ds(start, block), head_cols(h)]],
                [lambda h: cv_ref[pl.ds(start, block), head_cols(h)]],
                [mask],
                load,
                store,
            )
            return 0

        lax.fori_loop(0, (jnp.maximum(high - begin0, 0) + block - 1) // block, step, 0)
    for copy in copies:
        copy.wait()
    for r in range(reqs):
        fold_shards(q_ref, r, offset, kv_local, info[2, offset + r], bases, base0, held, groups, states)


def state_shapes(reqs, kv_local, rows):
    return [jax.ShapeDtypeStruct((reqs, kv_local, rows, HD), jnp.float32)] * 3


def shard_scratch(shards):
    n = 2 * len(shards)
    return [pltpu.VMEM((n,) + shards[0][0].shape, jnp.bfloat16), pltpu.SemaphoreType.DMA((n,))]


def flat(shards):
    return [k for k, _ in shards] + [v for _, v in shards]


def attend_first(parts, ancestry, cache_keys, cache_values, info, bases, shards, span, offset, reqs, after=()):
    queries, new_keys, new_values = parts
    shards = shards[span[0] : span[1]]
    _, n_heads, tree, _ = queries.shape
    capacity, cols = cache_keys.shape
    kv_local = cols // HD
    near = min(384 - tree, capacity)
    block = min(896, capacity)
    n = len(shards)
    return call(
        functools.partial(first_kernel, kv_local, near, block, n, offset, pairs_of(n), span[0]),
        [SMEM] * 2 + [VMEM] * 6 + [HBM] * (2 * n),
        [info, bases, queries, new_keys, new_values, ancestry, cache_keys, cache_values, *flat(shards)],
        state_shapes(reqs, kv_local, n_heads // kv_local * tree),
        [pltpu.VMEM((tree + near, cols), jnp.bfloat16)] * 2 + shard_scratch(shards),
        40,
        6,
        "attend_first",
        after,
    )


def middle_kernel(kv_local, n_shards, offset, groups, base0, info, bases, q_ref, *refs):
    sources = refs[: 2 * n_shards]
    ins = refs[2 * n_shards : 2 * n_shards + 3]
    outs = refs[2 * n_shards + 3 : 2 * n_shards + 6]
    held, sems = refs[2 * n_shards + 6 :]
    copies = fetch_all(sources, held, sems)
    for src, dst in zip(ins, outs):
        dst[...] = src[...]
    for copy in copies:
        copy.wait()
    for r in range(outs[0].shape[0]):
        fold_shards(q_ref, r, offset, kv_local, info[2, offset + r], bases, base0, held, groups, outs)


def attend_middle(queries, info, bases, shards, span, state, offset, after=()):
    shards = shards[span[0] : span[1]]
    reqs = state[0].shape[0]
    _, n_heads, tree, _ = queries.shape
    kv_local = shards[0][0].shape[1] // HD
    n = len(shards)
    return call(
        functools.partial(middle_kernel, kv_local, n, offset, pairs_of(n), span[0]),
        [SMEM] * 2 + [VMEM] + [HBM] * (2 * n) + [VMEM] * 3,
        [info, bases, queries, *flat(shards), *state],
        state_shapes(reqs, kv_local, n_heads // kv_local * tree),
        shard_scratch(shards),
        40,
        1.5 + 0.4 * n * reqs,
        "attend_middle",
        after,
    )


def last_kernel(kv_local, n_shards, offset, groups, base0, block, info, bases, q_ref, *refs):
    sources = refs[: 2 * n_shards]
    ins = refs[2 * n_shards : 2 * n_shards + 3]
    w_ref = refs[2 * n_shards + 3]
    m_s, l_s, acc_s, attended, w_held, w_sems, held, sems = refs[-8:]
    reqs = m_s.shape[0]
    n_heads, tree = q_ref.shape[1:3]
    outs = refs[-8 - reqs : -8]
    states = (m_s, l_s, acc_s)
    group = n_heads // kv_local
    copies = fetch_all(sources, held, sems)
    cuts = [slice(lo, lo + block) for lo in range(0, w_ref.shape[1], block)]
    w_copies = fetch_all([w_ref.at[:, cut] for cut in cuts], w_held, w_sems)
    for src, dst in zip(ins, states):
        dst[...] = src[...]
    for copy in copies:
        copy.wait()
    for r in range(reqs):
        fold_shards(q_ref, r, offset, kv_local, info[2, offset + r], bases, base0, held, groups, states)
        for h in range(kv_local):
            total = jnp.sum(l_s[r, h], axis=1, keepdims=True)
            result = (acc_s[r, h] / total).astype(jnp.bfloat16)
            for g in range(group):
                attended[r, :, head_cols(h * group + g)] = result[g * tree : (g + 1) * tree]
    x = attended[...].reshape(reqs * tree, n_heads * HD)
    for i, cut in enumerate(cuts):
        w_copies[i].wait()
        product = jnp.dot(x, w_held[i], preferred_element_type=jnp.float32).astype(jnp.bfloat16)
        for r in range(reqs):
            outs[r][:, cut] = product[r * tree : (r + 1) * tree]


def attend_last(queries, info, bases, shards, span, state, w_out, offset, after=()):
    shards = shards[span[0] : span[1]]
    reqs = state[0].shape[0]
    _, n_heads, tree, _ = queries.shape
    kv_local = shards[0][0].shape[1] // HD
    rows = n_heads // kv_local * tree
    n = len(shards)
    depth, width = w_out.shape
    block = min(1024, width)
    return call(
        functools.partial(last_kernel, kv_local, n, offset, pairs_of(n), span[0], block),
        [SMEM] * 2 + [VMEM] + [HBM] * (2 * n) + [VMEM] * 3 + [HBM],
        [info, bases, queries, *flat(shards), *state, w_out],
        [jax.ShapeDtypeStruct((tree, width), jnp.bfloat16)] * reqs,
        [pltpu.VMEM((reqs, kv_local, rows, HD), jnp.float32)] * 3
        + [
            pltpu.VMEM((reqs, tree, n_heads * HD), jnp.bfloat16),
            pltpu.VMEM((width // block, depth, block), jnp.bfloat16),
            pltpu.SemaphoreType.DMA((width // block,)),
        ]
        + shard_scratch(shards),
        50,
        3.5 + 0.4 * n * reqs,
        "attend_last",
        after,
    )


def add_kernel(*refs):
    total = refs[0][...].astype(jnp.float32)
    for ref in refs[1:-1]:
        total = total + ref[...].astype(jnp.float32)
    refs[-1][...] = total.astype(refs[-1].dtype)


def add_up(*terms, dtype=jnp.bfloat16):
    outs = call(
        add_kernel,
        [VMEM] * len(terms),
        list(terms),
        [jax.ShapeDtypeStruct(terms[0].shape, dtype)],
        [],
        8,
        1,
        "add_up",
    )
    return outs[0]


def ancestor_table(parents):
    node_count = parents.shape[-1]
    column = jnp.arange(node_count, dtype=jnp.int32)
    linked = (parents[..., None] == column) | (column[:, None] == column[None, :])
    ancestry = linked.astype(jnp.bfloat16)
    for repeat in range((node_count - 1).bit_length()):
        paths = jnp.einsum("rij,rjk->rik", ancestry, ancestry, preferred_element_type=jnp.float32)
        ancestry = jnp.minimum(paths, 1.0).astype(jnp.bfloat16)
    return ancestry.astype(jnp.float32)


def rotary_tables(position):
    half = HD // 2
    frequency = 10000.0 ** (-jnp.arange(half, dtype=jnp.float32) / half)
    angles = position.astype(jnp.float32)[:, None] * frequency[None, :]
    cosine = jnp.cos(angles)
    sine = jnp.sin(angles)
    return jnp.concatenate([cosine, cosine], axis=1), jnp.concatenate([-sine, sine], axis=1)


def swap_pairs(batch, tensor, move):
    columns = 2
    pairs = []
    for z in range(batch // columns):
        for x in range(columns):
            for t in range(tensor):
                z2, x2, t2 = move(z, x, t)
                pairs.append(((z * columns + x) * tensor + t, (z2 * columns + x2) * tensor + t2))
    return pairs


def body(
    sizes,
    tokens,
    norm_gain,
    w_query,
    w_key,
    w_value,
    w_out,
    prefix_keys,
    prefix_values,
    cache_keys,
    cache_values,
    cache_lengths,
    prefix_used,
    parents,
    accepted_index,
):
    batch, tensor = sizes
    reqs, tree = parents.shape
    shard_rows = prefix_keys.shape[0]
    fast = sizes == (8, 4) and reqs == tensor and tokens.shape[0] == tree
    me_batch = lax.axis_index("batch")
    me_tensor = lax.axis_index("tensor")
    slots = jnp.arange(reqs, dtype=jnp.int32)

    if fast:
        pairs = functools.partial(swap_pairs, batch, tensor)
        core_pairs = pairs(lambda z, x, t: (z, x, t ^ 1))
        y_pairs = pairs(lambda z, x, t: (z, x, t ^ 2))
        x_pairs = pairs(lambda z, x, t: (z, 1 - x, t))
        z_pairs = pairs(lambda z, x, t: ((z + 1) % (batch // 2), x, t))
        send = lambda a, p: lax.ppermute(a, AXES, p)
        core_tokens = send(tokens, core_pairs)
        y_tokens = send(tokens, y_pairs)
        far_tokens = send(y_tokens, core_pairs)
    order = slots ^ me_tensor if fast else slots
    pick = order[:, None] == slots[None, :]
    own_lengths = lax.dynamic_slice_in_dim(cache_lengths, me_batch * reqs, reqs)
    lower = jnp.cumsum(own_lengths) - own_lengths
    table = jnp.stack([lower, lower + own_lengths, prefix_used])
    info = jnp.sum(jnp.where(pick[None], table[:, None, :], 0), axis=2)
    tree_parents = jnp.sum(jnp.where(pick[:, :, None], parents[None], 0), axis=1)
    ancestry = ancestor_table(tree_parents)
    tree_depth = (jnp.sum(ancestry, axis=-1) - 1.0).astype(jnp.int32)
    position = ((info[2] + info[1] - info[0])[:, None] + tree_depth).reshape(reqs * tree)
    if fast:
        steps = batch // 2
        own_keys, own_values, _ = lax.optimization_barrier((prefix_keys, prefix_values, own_lengths))
        ring = [(prefix_keys, prefix_values)]
        ring.append((send(own_keys, z_pairs), send(own_values, z_pairs)))
        side = [(send(own_keys, x_pairs), send(own_values, x_pairs))]
    cosine, sine = rotary_tables(position)
    ancestry = jnp.pad(ancestry, ((0, 0), (0, 0), (0, HD - tree)))
    shard_ids = jnp.arange(batch, dtype=jnp.int32)
    if fast:
        z, x = me_batch // 2, me_batch % 2
        shard_ids = (z - shard_ids // 2) % (batch // 2) * 2 + (x ^ (shard_ids % 2))
    bases = (shard_ids * shard_rows).astype(jnp.int32)

    def projected(token_list, after=()):
        return project(token_list, norm_gain[None, :], cosine, sine, w_query, w_key, w_value, tree, after)

    if fast:
        def pass_on(step, after):
            keys, values, _ = lax.optimization_barrier((*ring[step], after))
            if step < steps - 1:
                ring.append((send(keys, z_pairs), send(values, z_pairs)))
                side.append((send(keys, x_pairs), send(values, x_pairs)))
            else:
                side.append((send(keys, x_pairs), send(side[-1][1], z_pairs)))

        pass_on(1, cosine)
        parts = projected([tokens, core_tokens, y_tokens, far_tokens])
        queries, new_keys, new_values = parts
        pass_on(2, queries)
        shards = [shard for s in range(steps - 1) for shard in (ring[s], side[s])]
        first = functools.partial(
            attend_first,
            (queries, new_keys, new_values),
            ancestry,
            cache_keys,
            cache_values,
            info,
            bases,
            shards,
            (0, 2),
            reqs=2,
        )
        far_state = first(offset=2)
        pass_on(steps - 1, far_state[0])
        shards += [ring[-1], side[-1]]
        n = len(shards)
        far_state = attend_middle(queries, info, bases, shards, (2, 5), far_state, 2)
        near_state = first(offset=0, after=far_state[:1])
        far_state = attend_middle(queries, info, bases, shards, (5, n - 1), far_state, 2, near_state[:1])
        kept, away = attend_last(queries, info, bases, shards, (n - 1, n), far_state, w_out, 2)
        got = send(away, core_pairs)
        summed = add_up(kept, got)
        far = send(summed, y_pairs)
        kept, away = attend_last(queries, info, bases, shards, (2, n), near_state, w_out, 0, (summed,))
        got = send(away, core_pairs)
        mixed_rows = add_up(add_up(kept, far, dtype=jnp.float32), got)
    else:
        gathered = lax.all_gather(tokens, "tensor", axis=0, tiled=True)
        parts = projected([gathered])
        queries, new_keys, new_values = parts
        all_keys = lax.all_gather(prefix_keys, "batch", axis=0, tiled=True)
        all_values = lax.all_gather(prefix_values, "batch", axis=0, tiled=True)
        split = lambda a: [a[i * shard_rows : (i + 1) * shard_rows] for i in range(batch)]
        shards = list(zip(split(all_keys), split(all_values)))
        state = attend_first(parts, ancestry, cache_keys, cache_values, info, bases, shards, (0, 2), 0, reqs)
        for s in range(2, batch - 2, 4):
            state = attend_middle(queries, info, bases, shards, (s, min(s + 4, batch - 2)), state, 0)
        partial = attend_last(queries, info, bases, shards, (batch - 2, batch), state, w_out, 0)
        mixed_rows = lax.psum_scatter(
            jnp.concatenate(partial, axis=0), "tensor", scatter_dimension=0, tiled=True
        )
    rows = ((slots ^ me_tensor if fast else slots)[:, None] * tree + accepted_index).reshape(-1)
    accepted_keys = jnp.take(new_keys, rows, axis=0).reshape(reqs, accepted_index.shape[1], -1)
    accepted_values = jnp.take(new_values, rows, axis=0).reshape(reqs, accepted_index.shape[1], -1)
    return (mixed_rows, accepted_keys, accepted_values)


def solution(mesh):
    sizes = (mesh.shape["batch"], mesh.shape["tensor"])
    in_specs = (
        P(("batch", "tensor"), None),
        P(),
        P(None, "tensor"),
        P(None, "tensor"),
        P(None, "tensor"),
        P("tensor", None),
        P("batch", "tensor"),
        P("batch", "tensor"),
        P("batch", "tensor"),
        P("batch", "tensor"),
        P(),
        P("batch"),
        P("batch", None),
        P("batch", None),
    )
    out_specs = (
        P(("batch", "tensor"), None),
        P("batch", None, "tensor"),
        P("batch", None, "tensor"),
    )
    return jax.shard_map(
        functools.partial(body, sizes), mesh=mesh, in_specs=in_specs, out_specs=out_specs, check_vma=False
    )
```

time: 202 us -> 93.7 us (0.46)
  matrix products: 60.1 us -> 1.15 us
  Pallas kernels: 0 us -> 40.3 us
  local copies, waits for them, and re-layouts: 38.8 us -> 9.23 us
  other arithmetic: 32.3 us -> 4.19 us
  loops' own time: 19.7 us -> 0 us
  starting transfers between devices: 0.16 us -> 18.9 us
  waiting for transfers between devices: 35.2 us -> 18.9 us
  between operations: 14.1 us -> 1 us
    dot_general x35 -> x3, matrix products: 60.1 us -> 1.15 us  [ancestor_table(): jnp.einsum('rij,rjk->rik', ancestry, ancestry, preferred_element_type=jnp...]
    pallas_call x0 -> x10, Pallas kernels: none -> 40.3 us  [call(): pl.pallas_call(wrapped, in_specs=in_specs + [HBM] * len(after), out_specs...]
    reduce_scatter x1 -> x0, waiting for transfers between devices: 27.4 us -> none  [body(): lax.psum_scatter(jnp.dot(attended, w_out, preferred_element_type=jnp.floa...]
    reduce_sum x13 -> x2, other arithmetic: 25.8 us -> 0.92 us  [the longest x1 0.78 us: body(): jnp.sum(jnp.where(pick[:, :, None], parents[None], 0), axis=1)]
    another operation x5 -> x0, loops' own time: 19.7 us -> none  [the longest x4 14.1 us: one_request(): return lax.fori_loop(0, blocks, block_step, start_carry)]
    ppermute x0 -> x20, waiting for transfers between devices: none -> 18.9 us  [body(): send = lambda a, p: lax.ppermute(a, AXES, p)]
    ppermute x0 -> x20, starting transfers between devices: none -> 18.9 us  [body(): send = lambda a, p: lax.ppermute(a, AXES, p)]
    dynamic_slice x18 -> x0, local copies, waits for them, and re-layouts: 18.5 us -> none  [the longest x10 13.5 us: block_step(): lax.dynamic_slice_in_dim(all_values, start, block_size, 0)]
  transfers between devices with their start and end apart: 4 -> 20, of which waited for: 3 -> 4; matrix products, arithmetic and copies ran while one was open for 52% -> 8% of each run, Pallas kernels for 0% -> 37%
where the time goes in v2:
time: 93.7 us
  Pallas kernels  40.3 us (43%)
  starting transfers between devices  18.9 us (20%)
  waiting for transfers between devices  18.9 us (20%)
  local copies, waits for them, and re-layouts  9.23 us (10%)
  other arithmetic  4.19 us (4%)
  matrix products  1.15 us (1%)
  between operations  1 us (1%)
    pallas_call x10, Pallas kernels, call(): pl.pallas_call(wrapped, in_specs=in_specs + [HBM] * len(after), out_specs...  40.3 us
    ppermute x20, waiting for transfers between devices, body(): send = lambda a, p: lax.ppermute(a, AXES, p)  18.9 us
    ppermute x20, starting transfers between devices, body(): send = lambda a, p: lax.ppermute(a, AXES, p)  18.9 us
    unnamed x52, local copies, waits for them, and re-layouts  7.07 us
  transfers between devices with their start and end apart: 20, of which 4 were waited for; matrix products, arithmetic and copies ran while one was open for 8% of the time, Pallas kernels for 37%

profile of v2, /device:TPU:0, one launch (start us, length us, event | category | flops | bytes accessed | tf_op | source)
XLA Modules:
  0.0 93.7 jit_solution(10825602344209368983)
XLA Ops:
  0.6 3.0 %collective-permute-start.11 = (bf16[512,256]{1,0:T(8,128)(2,1)}, bf16[512,256]{1,0:T(8,128)(2,1)S(1)}, u32[]{:S(2)}, u32[]{:S(2)}) collective-permute-start(bf16[512,256]{1,0:T(8,128)(2,1)} %refs_8_.6), channel_id=1, source_target_pairs={{0,4},{1,5},{2,6},{3,7},{4,0},{5,1},{6,2},{7,3},{8,12},{9,13},{10,... | collective-permute-start | bytes 786440 | tf_op jit(solution)/shard_map/ppermute | solution.py:502
  3.6 1.6 %collective-permute-start.3 = (bf16[512,256]{1,0:T(8,128)(2,1)}, bf16[512,256]{1,0:T(8,128)(2,1)S(1)}, u32[]{:S(2)}, u32[]{:S(2)}) collective-permute-start(bf16[512,256]{1,0:T(8,128)(2,1)} %refs_8_.6), channel_id=1, source_target_pairs={{0,8},{1,9},{2,10},{3,11},{4,12},{5,13},{6,14},{7,15},{8,16},{9,17... | collective-permute-start | bytes 786440 | tf_op jit(solution)/shard_map/ppermute | solution.py:502
  5.2 1.5 %collective-permute-start.1 = (bf16[64,4096]{1,0:T(8,128)(2,1)}, bf16[64,4096]{1,0:T(8,128)(2,1)S(1)}, u32[]{:S(2)}, u32[]{:S(2)}) collective-permute-start(bf16[64,4096]{1,0:T(8,128)(2,1)} %refs_0_.1), channel_id=1, source_target_pairs={{0,2},{1,3},{2,0},{3,1},{4,6},{5,7},{6,4},{7,5},{8,10},{9,11},{10,... | collective-permute-start | bytes 1572872 | tf_op jit(solution)/shard_map/ppermute | solution.py:502
  6.7 1.6 %collective-permute-start.4 = (bf16[512,256]{1,0:T(8,128)(2,1)}, bf16[512,256]{1,0:T(8,128)(2,1)S(1)}, u32[]{:S(2)}, u32[]{:S(2)}) collective-permute-start(bf16[512,256]{1,0:T(8,128)(2,1)} %refs_10_.3), channel_id=1, source_target_pairs={{0,8},{1,9},{2,10},{3,11},{4,12},{5,13},{6,14},{7,15},{8,16},{9,17... | collective-permute-start | bytes 786440 | tf_op jit(solution)/shard_map/ppermute | solution.py:502
  8.3 0.7 dynamic-slice_bitcast_fusion
  9.1 0.2 reduce-window.4
  9.2 0.7 fusion.24
  10.0 0.1 iota_compare_fusion.2
  10.1 0.7 pad_add_fusion
  10.7 0.1 select_reduce_fusion.1.refs_0_
  10.9 0.8 select_reduce_fusion
  11.6 0.5 fusion.1
  12.1 0.3 fusion.3
  12.4 0.4 fusion.28
  12.8 0.1 add_convert_fusion
  12.9 0.1 convert_element_type.52
  13.0 6.8 %collective-permute-done.1.refs_2_ = bf16[64,4096]{1,0:T(8,128)(2,1)S(1)} collective-permute-done((bf16[64,4096]{1,0:T(8,128)(2,1)}, bf16[64,4096]{1,0:T(8,128)(2,1)S(1)}, u32[]{:S(2)}, u32[]{:S(2)}) %collective-permute-start.1) | collective-permute-done | bytes 524320 | tf_op jit(solution)/shard_map/ppermute | solution.py:502
  19.8 0.0 collective-permute-start.2
  19.8 0.5 fusion.17
  20.3 0.1 pad_maximum_fusion.refs_5_
  20.5 0.1 pad_maximum_fusion.1.refs_6_
  20.6 0.0 collective-permute-done.3.refs_3_
  20.6 0.6 collective-permute-start.12
  21.2 1.6 %collective-permute-start.6 = (bf16[512,256]{1,0:T(8,128)(2,1)S(1)}, bf16[512,256]{1,0:T(8,128)(2,1)S(1)}, u32[]{:S(2)}, u32[]{:S(2)}) collective-permute-start(bf16[512,256]{1,0:T(8,128)(2,1)S(1)} %collective-permute-done.3.refs_3_), channel_id=1, source_target_pairs={{0,8},{1,9},{2,10},{3,11},{4,12},{5,13},{6,14},{7,15},{8,16},{9,17... | collective-permute-start | bytes 786440 | tf_op jit(solution)/shard_map/ppermute | solution.py:502
  22.8 0.0 collective-permute-done.refs_1_
  22.8 1.5 %collective-permute-start.5 = (bf16[512,256]{1,0:T(8,128)(2,1)S(1)}, bf16[512,256]{1,0:T(8,128)(2,1)S(1)}, u32[]{:S(2)}, u32[]{:S(2)}) collective-permute-start(bf16[512,256]{1,0:T(8,128)(2,1)S(1)} %collective-permute-done.3.refs_3_), channel_id=1, source_target_pairs={{0,4},{1,5},{2,6},{3,7},{4,0},{5,1},{6,2},{7,3},{8,12},{9,13},{10,... | collective-permute-start | bytes 786440 | tf_op jit(solution)/shard_map/ppermute | solution.py:502
  24.3 1.6 %collective-permute-start.7 = (bf16[512,256]{1,0:T(8,128)(2,1)S(1)}, bf16[512,256]{1,0:T(8,128)(2,1)S(1)}, u32[]{:S(2)}, u32[]{:S(2)}) collective-permute-start(bf16[512,256]{1,0:T(8,128)(2,1)S(1)} %collective-permute-done.4.refs_6_.refs_9_), channel_id=1, source_target_pairs={{0,8},{1,9},{2,10},{3,11},{4,12},{5,13},{6,14},{7,15},{8,16},{9,17... | collective-permute-start | bytes 786440 | tf_op jit(solution)/shard_map/ppermute | solution.py:502
  25.8 1.0 %copy-done.2 = bf16[64,4096]{1,0:T(8,128)(2,1)S(1)} copy-done((bf16[64,4096]{1,0:T(8,128)(2,1)S(1)}, bf16[64,4096]{1,0:T(8,128)(2,1)}, u32[]{:S(2)}) %copy-start.2) | copy-done | bytes 524312
  26.9 0.7 copy-done.16
  27.6 6.1 %project.1 = (bf16[4,8,64,128]{3,2,1,0:T(8,128)(2,1)S(1)}, bf16[256,256]{1,0:T(8,128)(2,1)S(1)}, bf16[256,256]{1,0:T(8,128)(2,1)S(1)}) custom-call(bf16[64,4096]{1,0:T(8,128)(2,1)S(1)} %copy-done.2, bf16[64,4096]{1,0:T(8,128)(2,1)S(1)} %collective-permute-done.refs_1_, bf16[64,4096]{1,0:T(8,128)(2,1)S(1)} %collective-permute-done.1.refs_2_, ...), custom_call_target="tpu_custom_call" | custom-call | flops 7699999744 | tf_op jit(solution)/shard_map/project/pallas_call | solution.py:27
  33.7 0.0 copy-start.21
  33.7 0.6 collective-permute-start.14
  34.3 2.8 %collective-permute-done.7.refs_8_.refs_11_ = bf16[512,256]{1,0:T(8,128)(2,1)S(1)} collective-permute-done((bf16[512,256]{1,0:T(8,128)(2,1)S(1)}, bf16[512,256]{1,0:T(8,128)(2,1)S(1)}, u32[]{:S(2)}, u32[]{:S(2)}) %collective-permute-start.7) | collective-permute-done | bytes 262176 | tf_op jit(solution)/shard_map/ppermute | solution.py:502
  37.0 1.5 %collective-permute-start.8 = (bf16[512,256]{1,0:T(8,128)(2,1)S(1)}, bf16[512,256]{1,0:T(8,128)(2,1)S(1)}, u32[]{:S(2)}, u32[]{:S(2)}) collective-permute-start(bf16[512,256]{1,0:T(8,128)(2,1)S(1)} %collective-permute-done.6.refs_5_), channel_id=1, source_target_pairs={{0,4},{1,5},{2,6},{3,7},{4,0},{5,1},{6,2},{7,3},{8,12},{9,13},{10,... | collective-permute-start | bytes 786440 | tf_op jit(solution)/shard_map/ppermute | solution.py:502
  38.5 0.5 collective-permute-start.15
  39.1 4.4 %attend_first.2 = (f32[2,2,256,128]{3,2,1,0:T(8,128)S(1)}, f32[2,2,256,128]{3,2,1,0:T(8,128)S(1)}, f32[2,2,256,128]{3,2,1,0:T(8,128)S(1)}) custom-call(s32[3,4]{1,0:T(4,128)S(1)} %select_reduce_fusion.1.refs_0_, s32[8]{0:T(128)S(1)} %fusion.20.refs_1_, bf16[4,8,64,128]{3,2,1,0:T(8,128)(2,1)S(1)} %get-tuple-element.30.refs_2_, ...), custom_call_target="tpu_custom_call" | custom-call | flops 6600000000 | tf_op jit(solution)/shard_map/attend_first/pallas_call | solution.py:27
  43.5 1.4 %collective-permute-start.10 = (bf16[512,256]{1,0:T(8,128)(2,1)S(1)}, bf16[512,256]{1,0:T(8,128)(2,1)S(1)}, u32[]{:S(2)}, u32[]{:S(2)}) collective-permute-start(bf16[512,256]{1,0:T(8,128)(2,1)S(1)} %collective-permute-done.7.refs_8_.refs_11_), channel_id=1, source_target_pairs={{0,8},{1,9},{2,10},{3,11},{4,12},{5,13},{6,14},{7,15},{8,16},{9,17... | collective-permute-start | bytes 786440 | tf_op jit(solution)/shard_map/ppermute | solution.py:502
  44.9 2.9 %attend_middle.2 = (f32[2,2,256,128]{3,2,1,0:T(8,128)S(1)}, f32[2,2,256,128]{3,2,1,0:T(8,128)S(1)}, f32[2,2,256,128]{3,2,1,0:T(8,128)S(1)}) custom-call(s32[3,4]{1,0:T(4,128)S(1)} %select_reduce_fusion.1.refs_0_, s32[8]{0:T(128)S(1)} %fusion.20.refs_1_, bf16[4,8,64,128]{3,2,1,0:T(8,128)(2,1)S(1)} %get-tuple-element.30.refs_2_, ...), custom_call_target="tpu_custom_call" | custom-call | flops 4289999872 | tf_op jit(solution)/shard_map/attend_middle/pallas_call | solution.py:27
  47.9 8.8 %attend_first.3 = (f32[2,2,256,128]{3,2,1,0:T(8,128)S(1)}, f32[2,2,256,128]{3,2,1,0:T(8,128)S(1)}, f32[2,2,256,128]{3,2,1,0:T(8,128)S(1)}) custom-call(s32[3,4]{1,0:T(4,128)S(1)} %select_reduce_fusion.1.refs_0_, s32[8]{0:T(128)S(1)} %fusion.20.refs_1_, bf16[4,8,64,128]{3,2,1,0:T(8,128)(2,1)S(1)} %get-tuple-element.30.refs_2_, ...), custom_call_target="tpu_custom_call" | custom-call | flops 6600000000 | tf_op jit(solution)/shard_map/attend_first/pallas_call | solution.py:27
  56.7 0.8 copy-done.23
  57.5 1.0 %collective-permute-start.13 = (bf16[512,256]{1,0:T(8,128)(2,1)S(1)}, bf16[512,256]{1,0:T(8,128)(2,1)S(1)}, u32[]{:S(2)}, u32[]{:S(2)}) collective-permute-start(bf16[512,256]{1,0:T(8,128)(2,1)S(1)} %collective-permute-done.9.refs_4_.refs_7_), channel_id=1, source_target_pairs={{0,4},{1,5},{2,6},{3,7},{4,0},{5,1},{6,2},{7,3},{8,12},{9,13},{10,... | collective-permute-start | bytes 786440 | tf_op jit(solution)/shard_map/ppermute | solution.py:502
  58.6 1.9 %attend_middle.3 = (f32[2,2,256,128]{3,2,1,0:T(8,128)S(1)}, f32[2,2,256,128]{3,2,1,0:T(8,128)S(1)}, f32[2,2,256,128]{3,2,1,0:T(8,128)S(1)}) custom-call(s32[3,4]{1,0:T(4,128)S(1)} %select_reduce_fusion.1.refs_0_, s32[8]{0:T(128)S(1)} %fusion.20.refs_1_, bf16[4,8,64,128]{3,2,1,0:T(8,128)(2,1)S(1)} %get-tuple-element.30.refs_2_, ...), custom_call_target="tpu_custom_call" | custom-call | flops 3409999872 | tf_op jit(solution)/shard_map/attend_middle/pallas_call | solution.py:27
  60.5 7.6 %collective-permute-done.16.refs_4_.refs_14_ = bf16[512,256]{1,0:T(8,128)(2,1)S(1)} collective-permute-done((bf16[512,256]{1,0:T(8,128)(2,1)S(1)}, bf16[512,256]{1,0:T(8,128)(2,1)S(1)}, u32[]{:S(2)}, u32[]{:S(2)}) %collective-permute-start.16) | collective-permute-done | bytes 262176 | tf_op jit(solution)/shard_map/ppermute | solution.py:502
  68.2 0.0 copy-start.25
  68.2 4.6 %attend_last.2 = (bf16[64,4096]{1,0:T(8,128)(2,1)S(1)}, bf16[64,4096]{1,0:T(8,128)(2,1)S(1)}) custom-call(s32[3,4]{1,0:T(4,128)S(1)} %select_reduce_fusion.1.refs_0_, s32[8]{0:T(128)S(1)} %fusion.20.refs_1_, bf16[4,8,64,128]{3,2,1,0:T(8,128)(2,1)S(1)} %get-tuple-element.30.refs_2_, bf16[512,256]{1,0:T(8,128)(2,1)S(1)} %collective-permute-done.13.refs_3_.refs_8_, ...), custom_call_target="tpu_custom_call" | custom-call | flops 4729999872 | tf_op jit(solution)/shard_map/attend_last/pallas_call | solution.py:27
  72.8 0.7 copy-done.12
  73.5 0.8 copy-done.19
  74.3 0.1 broadcast_add_fusion
  74.4 0.1 reshape.130
  74.5 1.7 %collective-permute-done.17.refs_1_ = bf16[64,4096]{1,0:T(8,128)(2,1)S(1)} collective-permute-done((bf16[64,4096]{1,0:T(8,128)(2,1)S(1)}, bf16[64,4096]{1,0:T(8,128)(2,1)S(1)}, u32[]{:S(2)}, u32[]{:S(2)}) %collective-permute-start.17) | collective-permute-done | bytes 524320 | tf_op jit(solution)/shard_map/ppermute | solution.py:502
  76.2 1.0 %copy-done.20 = bf16[64,4096]{1,0:T(8,128)(2,1)S(1)} copy-done((bf16[64,4096]{1,0:T(8,128)(2,1)S(1)}, bf16[64,4096]{1,0:T(8,128)(2,1)}, u32[]{:S(2)}) %copy-start.20) | copy-done | bytes 524312
  77.3 0.1 add_up.3.refs_19_
  77.4 0.7 collective-permute-start.18
  78.2 0.0 copy-done.3
  78.2 10.4 %attend_last.3 = (bf16[64,4096]{1,0:T(8,128)(2,1)S(1)}, bf16[64,4096]{1,0:T(8,128)(2,1)}) custom-call(s32[3,4]{1,0:T(4,128)S(1)} %select_reduce_fusion.1.refs_0_, s32[8]{0:T(128)S(1)} %fusion.20.refs_1_, bf16[4,8,64,128]{3,2,1,0:T(8,128)(2,1)} %copy-done.21, bf16[512,256]{1,0:T(8,128)(2,1)S(1)} %collective-permute-done.3.refs_3_, ...), custom_call_target="tpu_custom_call" | custom-call | flops 9130000384 | tf_op jit(solution)/shard_map/attend_last/pallas_call | solution.py:27
  88.7 0.0 copy-start.17
  88.7 0.8 copy-done.17
  89.5 0.1 collective-permute-start.19
  89.6 0.6 gather_fusion
  90.2 0.6 gather_fusion.1
  90.9 0.7 select_bitcast_fusion
  91.6 1.0 %copy-done.18 = bf16[64,4096]{1,0:T(8,128)(2,1)S(1)} copy-done((bf16[64,4096]{1,0:T(8,128)(2,1)S(1)}, bf16[64,4096]{1,0:T(8,128)(2,1)}, u32[]{:S(2)}) %copy-start.18) | copy-done | bytes 524312
  92.6 0.1 add_up.4.refs_0_
  92.7 0.9 add_up.5
  (67 shorter events, 0.2 us)
Async XLA Ops:
  0.6 36.4 %collective-permute-start.11 = (bf16[512,256]{1,0:T(8,128)(2,1)}, bf16[512,256]{1,0:T(8,128)(2,1)S(1)}, u32[]{:S(2)}, u32[]{:S(2)}) collective-permute-start(bf16[512,256]{1,0:T(8,128)(2,1)} %refs_8_.6), channel_id=1, source_target_pairs={{0,4},{1,5},{2,6},{3,7},{4,0},{5,1},{6,2},{7,3},{8,12},{9,13},{10,... | collective-permute-start | bytes 786440 | tf_op jit(solution)/shard_map/ppermute | solution.py:502
  3.6 16.9 %collective-permute-start.3 = (bf16[512,256]{1,0:T(8,128)(2,1)}, bf16[512,256]{1,0:T(8,128)(2,1)S(1)}, u32[]{:S(2)}, u32[]{:S(2)}) collective-permute-start(bf16[512,256]{1,0:T(8,128)(2,1)} %refs_8_.6), channel_id=1, source_target_pairs={{0,8},{1,9},{2,10},{3,11},{4,12},{5,13},{6,14},{7,15},{8,16},{9,17... | collective-permute-start | bytes 786440 | tf_op jit(solution)/shard_map/ppermute | solution.py:502
  5.2 17.5 %collective-permute-start = (bf16[64,4096]{1,0:T(8,128)(2,1)}, bf16[64,4096]{1,0:T(8,128)(2,1)S(1)}, u32[]{:S(2)}, u32[]{:S(2)}) collective-permute-start(bf16[64,4096]{1,0:T(8,128)(2,1)} %refs_0_.1), channel_id=1, source_target_pairs={{0,1},{1,0},{2,3},{3,2},{4,5},{5,4},{6,7},{7,6},{8,9},{9,8},{10,11... | collective-permute-start | bytes 1572872 | tf_op jit(solution)/shard_map/ppermute | solution.py:502
  5.2 14.5 %collective-permute-start.1 = (bf16[64,4096]{1,0:T(8,128)(2,1)}, bf16[64,4096]{1,0:T(8,128)(2,1)S(1)}, u32[]{:S(2)}, u32[]{:S(2)}) collective-permute-start(bf16[64,4096]{1,0:T(8,128)(2,1)} %refs_0_.1), channel_id=1, source_target_pairs={{0,2},{1,3},{2,0},{3,1},{4,6},{5,7},{6,4},{7,5},{8,10},{9,11},{10,... | collective-permute-start | bytes 1572872 | tf_op jit(solution)/shard_map/ppermute | solution.py:502
  6.7 14.4 %collective-permute-start.4 = (bf16[512,256]{1,0:T(8,128)(2,1)}, bf16[512,256]{1,0:T(8,128)(2,1)S(1)}, u32[]{:S(2)}, u32[]{:S(2)}) collective-permute-start(bf16[512,256]{1,0:T(8,128)(2,1)} %refs_10_.3), channel_id=1, source_target_pairs={{0,8},{1,9},{2,10},{3,11},{4,12},{5,13},{6,14},{7,15},{8,16},{9,17... | collective-permute-start | bytes 786440 | tf_op jit(solution)/shard_map/ppermute | solution.py:502
  19.8 4.5 %collective-permute-start.2 = (bf16[64,4096]{1,0:T(8,128)(2,1)S(1)}, bf16[64,4096]{1,0:T(8,128)(2,1)S(1)}, u32[]{:S(2)}, u32[]{:S(2)}) collective-permute-start(bf16[64,4096]{1,0:T(8,128)(2,1)S(1)} %collective-permute-done.1.refs_2_), channel_id=1, source_target_pairs={{0,1},{1,0},{2,3},{3,2},{4,5},{5,4},{6,7},{7,6},{8,9},{9,8},{10,11... | collective-permute-start | bytes 1572872 | tf_op jit(solution)/shard_map/ppermute | solution.py:502
  20.6 18.0 %collective-permute-start.12 = (bf16[512,256]{1,0:T(8,128)(2,1)}, bf16[512,256]{1,0:T(8,128)(2,1)S(1)}, u32[]{:S(2)}, u32[]{:S(2)}) collective-permute-start(bf16[512,256]{1,0:T(8,128)(2,1)} %refs_10_.3), channel_id=1, source_target_pairs={{0,4},{1,5},{2,6},{3,7},{4,0},{5,1},{6,2},{7,3},{8,12},{9,13},{10,... | collective-permute-start | bytes 786440 | tf_op jit(solution)/shard_map/ppermute | solution.py:502
  21.2 12.5 %collective-permute-start.6 = (bf16[512,256]{1,0:T(8,128)(2,1)S(1)}, bf16[512,256]{1,0:T(8,128)(2,1)S(1)}, u32[]{:S(2)}, u32[]{:S(2)}) collective-permute-start(bf16[512,256]{1,0:T(8,128)(2,1)S(1)} %collective-permute-done.3.refs_3_), channel_id=1, source_target_pairs={{0,8},{1,9},{2,10},{3,11},{4,12},{5,13},{6,14},{7,15},{8,16},{9,17... | collective-permute-start | bytes 786440 | tf_op jit(solution)/shard_map/ppermute | solution.py:502
  22.8 20.8 %collective-permute-start.5 = (bf16[512,256]{1,0:T(8,128)(2,1)S(1)}, bf16[512,256]{1,0:T(8,128)(2,1)S(1)}, u32[]{:S(2)}, u32[]{:S(2)}) collective-permute-start(bf16[512,256]{1,0:T(8,128)(2,1)S(1)} %collective-permute-done.3.refs_3_), channel_id=1, source_target_pairs={{0,4},{1,5},{2,6},{3,7},{4,0},{5,1},{6,2},{7,3},{8,12},{9,13},{10,... | collective-permute-start | bytes 786440 | tf_op jit(solution)/shard_map/ppermute | solution.py:502
  24.3 12.8 %collective-permute-start.7 = (bf16[512,256]{1,0:T(8,128)(2,1)S(1)}, bf16[512,256]{1,0:T(8,128)(2,1)S(1)}, u32[]{:S(2)}, u32[]{:S(2)}) collective-permute-start(bf16[512,256]{1,0:T(8,128)(2,1)S(1)} %collective-permute-done.4.refs_6_.refs_9_), channel_id=1, source_target_pairs={{0,8},{1,9},{2,10},{3,11},{4,12},{5,13},{6,14},{7,15},{8,16},{9,17... | collective-permute-start | bytes 786440 | tf_op jit(solution)/shard_map/ppermute | solution.py:502
  25.8 1.0 %copy-start.2 = (bf16[64,4096]{1,0:T(8,128)(2,1)S(1)}, bf16[64,4096]{1,0:T(8,128)(2,1)}, u32[]{:S(2)}) copy-start(bf16[64,4096]{1,0:T(8,128)(2,1)} %refs_0_.1) | copy-start | bytes 1572868
  26.9 0.7 copy-start.16
  27.6 11.5 %copy-start = (bf16[4608,256]{1,0:T(8,128)(2,1)S(1)}, bf16[4608,256]{1,0:T(8,128)(2,1)}, u32[]{:S(2)}) copy-start(bf16[4608,256]{1,0:T(8,128)(2,1)} %refs_6_.3) | copy-start | bytes 7077892
  27.6 11.5 %copy-start.1 = (bf16[4608,256]{1,0:T(8,128)(2,1)S(1)}, bf16[4608,256]{1,0:T(8,128)(2,1)}, u32[]{:S(2)}) copy-start(bf16[4608,256]{1,0:T(8,128)(2,1)} %refs_7_.5) | copy-start | bytes 7077892
  27.6 11.5 %copy-start.4 = (bf16[512,256]{1,0:T(8,128)(2,1)S(1)}, bf16[512,256]{1,0:T(8,128)(2,1)}, u32[]{:S(2)}) copy-start(bf16[512,256]{1,0:T(8,128)(2,1)} %refs_8_.6) | copy-start | bytes 786436
  27.6 11.5 %copy-start.5 = (bf16[512,256]{1,0:T(8,128)(2,1)S(1)}, bf16[512,256]{1,0:T(8,128)(2,1)}, u32[]{:S(2)}) copy-start(bf16[512,256]{1,0:T(8,128)(2,1)} %refs_10_.3) | copy-start | bytes 786436
  33.7 34.5 %copy-start.21 = (bf16[4,8,64,128]{3,2,1,0:T(8,128)(2,1)}, bf16[4,8,64,128]{3,2,1,0:T(8,128)(2,1)S(1)}, u32[]{:S(2)}) copy-start(bf16[4,8,64,128]{3,2,1,0:T(8,128)(2,1)S(1)} %get-tuple-element.30.refs_2_) | copy-start | bytes 1572868
  33.7 11.2 %collective-permute-start.14 = (bf16[512,256]{1,0:T(8,128)(2,1)S(1)}, bf16[512,256]{1,0:T(8,128)(2,1)S(1)}, u32[]{:S(2)}, u32[]{:S(2)}) collective-permute-start(bf16[512,256]{1,0:T(8,128)(2,1)S(1)} %collective-permute-done.4.refs_6_.refs_9_), channel_id=1, source_target_pairs={{0,4},{1,5},{2,6},{3,7},{4,0},{5,1},{6,2},{7,3},{8,12},{9,13},{10,... | collective-permute-start | bytes 786440 | tf_op jit(solution)/shard_map/ppermute | solution.py:502
  37.0 20.5 %collective-permute-start.9 = (bf16[512,256]{1,0:T(8,128)(2,1)S(1)}, bf16[512,256]{1,0:T(8,128)(2,1)S(1)}, u32[]{:S(2)}, u32[]{:S(2)}) collective-permute-start(bf16[512,256]{1,0:T(8,128)(2,1)S(1)} %collective-permute-done.6.refs_5_), channel_id=1, source_target_pairs={{0,8},{1,9},{2,10},{3,11},{4,12},{5,13},{6,14},{7,15},{8,16},{9,17... | collective-permute-start | bytes 786440 | tf_op jit(solution)/shard_map/ppermute | solution.py:502
  37.0 21.5 %collective-permute-start.8 = (bf16[512,256]{1,0:T(8,128)(2,1)S(1)}, bf16[512,256]{1,0:T(8,128)(2,1)S(1)}, u32[]{:S(2)}, u32[]{:S(2)}) collective-permute-start(bf16[512,256]{1,0:T(8,128)(2,1)S(1)} %collective-permute-done.6.refs_5_), channel_id=1, source_target_pairs={{0,4},{1,5},{2,6},{3,7},{4,0},{5,1},{6,2},{7,3},{8,12},{9,13},{10,... | collective-permute-start | bytes 786440 | tf_op jit(solution)/shard_map/ppermute | solution.py:502
  38.5 20.0 %collective-permute-start.15 = (bf16[512,256]{1,0:T(8,128)(2,1)S(1)}, bf16[512,256]{1,0:T(8,128)(2,1)S(1)}, u32[]{:S(2)}, u32[]{:S(2)}) collective-permute-start(bf16[512,256]{1,0:T(8,128)(2,1)S(1)} %collective-permute-done.7.refs_8_.refs_11_), channel_id=1, source_target_pairs={{0,4},{1,5},{2,6},{3,7},{4,0},{5,1},{6,2},{7,3},{8,12},{9,13},{10,... | collective-permute-start | bytes 786440 | tf_op jit(solution)/shard_map/ppermute | solution.py:502
  43.5 14.0 %collective-permute-start.10 = (bf16[512,256]{1,0:T(8,128)(2,1)S(1)}, bf16[512,256]{1,0:T(8,128)(2,1)S(1)}, u32[]{:S(2)}, u32[]{:S(2)}) collective-permute-start(bf16[512,256]{1,0:T(8,128)(2,1)S(1)} %collective-permute-done.7.refs_8_.refs_11_), channel_id=1, source_target_pairs={{0,8},{1,9},{2,10},{3,11},{4,12},{5,13},{6,14},{7,15},{8,16},{9,17... | collective-permute-start | bytes 786440 | tf_op jit(solution)/shard_map/ppermute | solution.py:502
  56.7 0.8 copy-start.23
  57.5 3.0 %copy-start.22 = (f32[2,2,256,128]{3,2,1,0:T(8,128)}, f32[2,2,256,128]{3,2,1,0:T(8,128)S(1)}, u32[]{:S(2)}) copy-start(f32[2,2,256,128]{3,2,1,0:T(8,128)S(1)} %get-tuple-element.44.refs_10_.refs_15_) | copy-start | bytes 1572868
  57.5 3.0 %copy-start.24 = (f32[2,2,256,128]{3,2,1,0:T(8,128)}, f32[2,2,256,128]{3,2,1,0:T(8,128)S(1)}, u32[]{:S(2)}) copy-start(f32[2,2,256,128]{3,2,1,0:T(8,128)S(1)} %get-tuple-element.46.refs_17_) | copy-start | bytes 1572868
  57.5 3.0 %copy-start.10 = (bf16[512,256]{1,0:T(8,128)(2,1)}, bf16[512,256]{1,0:T(8,128)(2,1)S(1)}, u32[]{:S(2)}) copy-start(bf16[512,256]{1,0:T(8,128)(2,1)S(1)} %collective-permute-done.10.refs_6_.refs_13_) | copy-start | bytes 786436
  57.5 10.7 %collective-permute-start.13 = (bf16[512,256]{1,0:T(8,128)(2,1)S(1)}, bf16[512,256]{1,0:T(8,128)(2,1)S(1)}, u32[]{:S(2)}, u32[]{:S(2)}) collective-permute-start(bf16[512,256]{1,0:T(8,128)(2,1)S(1)} %collective-permute-done.9.refs_4_.refs_7_), channel_id=1, source_target_pairs={{0,4},{1,5},{2,6},{3,7},{4,0},{5,1},{6,2},{7,3},{8,12},{9,13},{10,... | collective-permute-start | bytes 786440 | tf_op jit(solution)/shard_map/ppermute | solution.py:502
  58.6 2.0 %copy-start.8 = (bf16[512,256]{1,0:T(8,128)(2,1)}, bf16[512,256]{1,0:T(8,128)(2,1)S(1)}, u32[]{:S(2)}) copy-start(bf16[512,256]{1,0:T(8,128)(2,1)S(1)} %collective-permute-done.15.refs_5_.refs_12_) | copy-start | bytes 786436
  58.6 9.6 %collective-permute-start.16 = (bf16[512,256]{1,0:T(8,128)(2,1)S(1)}, bf16[512,256]{1,0:T(8,128)(2,1)S(1)}, u32[]{:S(2)}, u32[]{:S(2)}) collective-permute-start(bf16[512,256]{1,0:T(8,128)(2,1)S(1)} %collective-permute-done.15.refs_5_.refs_12_), channel_id=1, source_target_pairs={{0,8},{1,9},{2,10},{3,11},{4,12},{5,13},{6,14},{7,15},{8,16},{9,17... | collective-permute-start | bytes 786440 | tf_op jit(solution)/shard_map/ppermute | solution.py:502
  58.6 2.0 %copy-start.6 = (bf16[512,256]{1,0:T(8,128)(2,1)}, bf16[512,256]{1,0:T(8,128)(2,1)S(1)}, u32[]{:S(2)}) copy-start(bf16[512,256]{1,0:T(8,128)(2,1)S(1)} %collective-permute-done.8.refs_3_.refs_6_) | copy-start | bytes 786436
  68.2 4.6 %copy-start.14 = (bf16[512,256]{1,0:T(8,128)(2,1)}, bf16[512,256]{1,0:T(8,128)(2,1)S(1)}, u32[]{:S(2)}) copy-start(bf16[512,256]{1,0:T(8,128)(2,1)S(1)} %collective-permute-done.16.refs_4_.refs_14_) | copy-start | bytes 786436
  68.2 6.1 %copy-start.25 = (s32[4,8]{1,0:T(4,128)S(1)}, s32[4,8]{1,0:T(4,128)}, u32[]{:S(2)}) copy-start(s32[4,8]{1,0:T(4,128)} %param.29) | copy-start | bytes 388
  72.8 0.7 copy-start.12
  73.5 0.8 copy-start.19
  74.3 3.9 %copy-start.7 = (bf16[512,256]{1,0:T(8,128)(2,1)S(1)}, bf16[512,256]{1,0:T(8,128)(2,1)}, u32[]{:S(2)}) copy-start(bf16[512,256]{1,0:T(8,128)(2,1)} %copy-done.6) | copy-start | bytes 786436
  74.3 1.9 %collective-permute-start.17 = (bf16[64,4096]{1,0:T(8,128)(2,1)S(1)}, bf16[64,4096]{1,0:T(8,128)(2,1)S(1)}, u32[]{:S(2)}, u32[]{:S(2)}) collective-permute-start(bf16[64,4096]{1,0:T(8,128)(2,1)S(1)} %get-tuple-element.53), channel_id=1, source_target_pairs={{0,1},{1,0},{2,3},{3,2},{4,5},{5,4},{6,7},{7,6},{8,9},{9,8},{10,11... | collective-permute-start | bytes 1572872 | tf_op jit(solution)/shard_map/ppermute | solution.py:502
  74.5 3.7 %copy-start.9 = (bf16[512,256]{1,0:T(8,128)(2,1)S(1)}, bf16[512,256]{1,0:T(8,128)(2,1)}, u32[]{:S(2)}) copy-start(bf16[512,256]{1,0:T(8,128)(2,1)} %copy-done.8) | copy-start | bytes 786436
  74.5 3.7 %copy-start.11 = (bf16[512,256]{1,0:T(8,128)(2,1)S(1)}, bf16[512,256]{1,0:T(8,128)(2,1)}, u32[]{:S(2)}) copy-start(bf16[512,256]{1,0:T(8,128)(2,1)} %copy-done.10) | copy-start | bytes 786436
  74.5 3.7 %copy-start.13 = (bf16[512,256]{1,0:T(8,128)(2,1)S(1)}, bf16[512,256]{1,0:T(8,128)(2,1)}, u32[]{:S(2)}) copy-start(bf16[512,256]{1,0:T(8,128)(2,1)} %copy-done.12) | copy-start | bytes 786436
  74.5 3.7 %copy-start.15 = (bf16[512,256]{1,0:T(8,128)(2,1)S(1)}, bf16[512,256]{1,0:T(8,128)(2,1)}, u32[]{:S(2)}) copy-start(bf16[512,256]{1,0:T(8,128)(2,1)} %copy-done.14) | copy-start | bytes 786436
  76.2 1.0 %copy-start.20 = (bf16[64,4096]{1,0:T(8,128)(2,1)S(1)}, bf16[64,4096]{1,0:T(8,128)(2,1)}, u32[]{:S(2)}) copy-start(bf16[64,4096]{1,0:T(8,128)(2,1)} %copy-done.19) | copy-start | bytes 1572868
  77.4 0.8 copy-start.3
  77.4 14.1 %collective-permute-start.18 = (bf16[64,4096]{1,0:T(8,128)(2,1)S(1)}, bf16[64,4096]{1,0:T(8,128)(2,1)S(1)}, u32[]{:S(2)}, u32[]{:S(2)}) collective-permute-start(bf16[64,4096]{1,0:T(8,128)(2,1)S(1)} %add_up.3.refs_19_), channel_id=1, source_target_pairs={{0,2},{1,3},{2,0},{3,1},{4,6},{5,7},{6,4},{7,5},{8,10},{9,11},{10,... | collective-permute-start | bytes 1572872 | tf_op jit(solution)/shard_map/ppermute | solution.py:502
  88.7 0.8 copy-start.17
  89.5 3.3 %collective-permute-start.19 = (bf16[64,4096]{1,0:T(8,128)(2,1)}, bf16[64,4096]{1,0:T(8,128)(2,1)S(1)}, u32[]{:S(2)}, u32[]{:S(2)}) collective-permute-start(bf16[64,4096]{1,0:T(8,128)(2,1)} %get-tuple-element.55), channel_id=1, source_target_pairs={{0,1},{1,0},{2,3},{3,2},{4,5},{5,4},{6,7},{7,6},{8,9},{9,8},{10,11... | collective-permute-start | bytes 1572872 | tf_op jit(solution)/shard_map/ppermute | solution.py:502
  91.6 1.0 %copy-start.18 = (bf16[64,4096]{1,0:T(8,128)(2,1)S(1)}, bf16[64,4096]{1,0:T(8,128)(2,1)}, u32[]{:S(2)}) copy-start(bf16[64,4096]{1,0:T(8,128)(2,1)} %copy-done.17) | copy-start | bytes 1572868
